TPU v7x, 256 devices: a whole 4x4x8 slice. The times are simulated.
256 devices in a mesh: group: 8 (over x, core), sub: 32 (over y, z).
Axes of the slice: x: 4, y: 4, z: 8, core: 2. Of those that a mesh axis runs over, the one named last changes fastest.
Arguments:
- resid_iface: float32 [256, 16, 4352], P(('group', 'sub')), may hold values from -6 to 6
- resid_inner: float32 [256, 16, 3072], P(('group', 'sub')), may hold values from -6 to 6
- weights: float32 [256, 4352], P(('group', 'sub')), may hold values from 0.25 to 0.75
- nbr: int32 [256, 32], P(('group', 'sub')), may hold values from 0 to 1, as said below
- own2: int32 [256, 128], P(('group', 'sub')), may hold values from 0 to 2047
- cidx: int32 [256, 8], P(('group', 'sub')), may hold values from 0 to 16
- neumann: bfloat16 [256, 17, 256, 256], P(('group', 'sub'))
- dirichlet: bfloat16 [256, 8, 384, 384], P(('group', 'sub'))
- coupling: bfloat16 [256, 8, 256, 384], P(('group', 'sub')), may hold values from -0.375 to 0.375
- coarse_basis: bfloat16 [256, 4352, 128], P(('group', 'sub')), may hold values from -0.5 to 0.5
- group_basis: float32 [16384, 512], P(('group', 'sub')), may hold values from -0.25 to 0.25
- group_inverse: float32 [16384, 2048], P('group', 'sub'), as said below
- top_inverse: float32 [512, 512], replicated, as said below
Outputs:
- interface_out: float32 [256, 16, 4352], P(('group', 'sub'))
- interior_out: float32 [256, 16, 3072], P(('group', 'sub'))
Inputs may be any that keep to these rules, and one draw needn't show every extreme that they name: Symmetric within each group (nbr[(g, q), j] = nbr[(g, j), q]) with nbr[(g, q), q] = 0. `group_inverse`: each matrix of a group is symmetric. `top_inverse`: symmetric.
All inputs are finite; a program needn't handle non-finite values.
Results may differ from a plain program's by a relative error of at most 0.013.
Values may be sent and summed in bfloat16 or wider, within the bound.
A program may use at most 64 MiB of HBM per device.

v0:
```python
import jax
import jax.numpy as jnp
from jax import lax
from jax.sharding import PartitionSpec as P


def padded_2(cells, sides, width):
    for axis, dim in sides:
        count = lax.axis_size(axis)
        ends = count - 1
        head = lax.slice_in_dim(cells, 0, width, axis=dim)
        tail = lax.slice_in_dim(cells, cells.shape[dim] - width, cells.shape[dim], axis=dim)
        cells = jnp.concatenate(
            [
                lax.ppermute(tail, axis, [(i, (i + 1) % count) for i in range(ends)]),
                cells,
                lax.ppermute(head, axis, [((i + 1) % count, i) for i in range(ends)]),
            ],
            axis=dim,
        )
    return cells


def shards(
    resid_iface,
    resid_inner,
    weights,
    nbr,
    own2,
    cidx,
    neumann,
    dirichlet,
    coupling,
    coarse_basis,
    group_basis,
    group_inverse,
    top_inverse,
):
    highest = lax.Precision.HIGHEST
    nsub = lax.axis_size("sub")
    mine = lax.axis_index("sub")
    rows = resid_iface.shape[1]
    width = resid_iface.shape[2]
    slot_width = width // (nsub + 2)
    block_count = neumann.shape[1]
    block_width = neumann.shape[2]
    inner_count = dirichlet.shape[1]
    inner_width = dirichlet.shape[2]
    group_width = group_inverse.shape[0]
    share = group_inverse.shape[1]
    slot_mask = jnp.concatenate([nbr[0].astype(jnp.float32), jnp.ones((2,), jnp.float32)])
    scale = jnp.repeat(slot_mask, slot_width) * weights[0]
    weighted = (scale[None, :] * resid_iface[0]).astype(jnp.bfloat16)
    local0 = jnp.dot(weighted, coarse_basis[0], preferred_element_type=jnp.float32)
    onehot = (own2[0][:, None] == jnp.arange(group_width, dtype=jnp.int32)[None, :]).astype(
        jnp.float32
    )
    contrib = jnp.dot(local0, onehot, precision=highest)
    level2 = lax.psum(contrib.astype(jnp.bfloat16), "sub").astype(jnp.float32)
    level2_mine = lax.dynamic_slice_in_dim(level2, mine * share, share, 1)
    neumann_part = jnp.einsum(
        "rkb,kbc->rkc",
        weighted.reshape(rows, block_count, block_width),
        neumann[0],
        preferred_element_type=jnp.float32,
    ).reshape(rows, width)
    top_term = jnp.dot(level2_mine, group_basis, precision=highest)
    level3 = lax.psum(top_term, ("group", "sub"))
    coarse3 = jnp.dot(level3, top_inverse, precision=highest)
    lifted = lax.dot_general(coarse3, group_basis, (((1,), (1,)), ((), ())), precision=highest)
    coarse2_mine = jnp.dot(level2, group_inverse, precision=highest) + lifted
    coarse2 = lax.all_gather(coarse2_mine.astype(jnp.bfloat16), "sub", axis=1, tiled=True)
    values = jnp.take(coarse2, own2[0], axis=1)
    spread = lax.dot_general(
        values, coarse_basis[0], (((1,), (1,)), ((), ())), preferred_element_type=jnp.float32
    )
    scaled = scale[None, :] * (neumann_part + spread)
    slots = scaled.reshape(rows, nsub + 2, slot_width)
    received = lax.all_to_all(
        slots[:, :nsub, :].astype(jnp.bfloat16), "sub", split_axis=1, concat_axis=1, tiled=True
    ).astype(jnp.float32)
    padded = padded_2(slots[:, nsub:, :], (("group", 1),), 1)
    lower_face = slots[:, nsub, :] + padded[:, 0, :]
    upper_face = slots[:, nsub + 1, :] + padded[:, 3, :]
    total = jnp.concatenate(
        [slots[:, :nsub, :] + received, lower_face[:, None, :], upper_face[:, None, :]], axis=1
    )
    interface_out = total.reshape(rows, width)
    iface_blocks = interface_out.reshape(rows, block_count, block_width).astype(jnp.bfloat16)
    picked = jnp.take(iface_blocks, cidx[0], axis=1)
    pushed = jnp.einsum("rkb,kbc->rkc", picked, coupling[0], preferred_element_type=jnp.float32)
    inner_rhs = (resid_inner[0].reshape(rows, inner_count, inner_width) - pushed).astype(
        jnp.bfloat16
    )
    interior_out = jnp.einsum(
        "rkb,kbc->rkc", inner_rhs, dirichlet[0], preferred_element_type=jnp.float32
    ).reshape(rows, inner_count * inner_width)
    return (interface_out[None], interior_out[None])


def solution(mesh):
    placed = (
        P(("group", "sub"), None, None),
        P(("group", "sub"), None, None),
        P(("group", "sub"), None),
        P(("group", "sub"), None),
        P(("group", "sub"), None),
        P(("group", "sub"), None),
        P(("group", "sub"), None, None, None),
        P(("group", "sub"), None, None, None),
        P(("group", "sub"), None, None, None),
        P(("group", "sub"), None, None),
        P(("group", "sub"), None),
        P("group", "sub"),
        P(),
    )
    return jax.shard_map(
        shards,
        mesh=mesh,
        in_specs=placed,
        out_specs=(P(("group", "sub"), None, None), P(("group", "sub"), None, None)),
        check_vma=False,
    )
```

profile of v0, /device:TPU:32, one launch (start us, length us, event | category | flops | bytes accessed | tf_op | source)
XLA Modules:
  0.0 317.0 jit_solution(4623421728509135453)
XLA Ops:
  7.2 0.0 all-reduce.3.cloned.1.call-start
  7.3 0.8 convert_bitcast_fusion
  8.1 0.1 broadcast_bitcast_fusion
  8.1 0.8 fusion.45
  8.9 1.6 fusion.25
  10.5 1.8 convolution_convert_fusion
  12.3 0.0 all-reduce.3.cloned.1.call-update
  12.6 2.0 fusion.7
  14.6 0.7 copy.43
  15.3 138.5 %all-reduce.3.cloned.1.call-done = bf16[16,2048]{1,0:T(8,128)(2,1)} async-done(((bf16[16,2048]{1,0:T(8,128)(2,1)}), bf16[16,2048]{1,0:T(8,128)(2,1)}) %all-reduce.3.cloned.1.call-update) | async-done | bytes 65552 | tf_op jit(solution)/shard_map/psum | solution.py:59
  153.9 1.7 fusion.47
  155.6 74.5 %psum.15 = f32[16,512]{1,0:T(8,128)S(1)} all-reduce(f32[16,512]{1,0:T(8,128)} %fusion.47), channel_id=1, replica_groups=mesh['group'=8,'sub'=32] {'group','sub'}, use_global_device_ids=true, to_apply=%region_1.0 | all-reduce | flops 8192 | bytes 65536 | tf_op jit(solution)/shard_map/psum | solution.py:68
  230.1 1.9 fusion.58
  232.0 1.4 fusion.57
  233.5 0.2 fusion.28
  233.7 43.7 %all-gather = bf16[32,64,16]{1,2,0:T(8,128)(2,1)} all-gather(bf16[1,64,16]{1,2,0:T(8,128)(2,1)S(1)} %fusion.28), channel_id=1, replica_groups=mesh['group'=8,'sub'=32] {'sub'}, dimensions={0}, use_global_device_ids=true | all-gather | bytes 67584 | tf_op jit(solution)/shard_map/all_gather | solution.py:72
  277.4 1.9 copy.41
  279.3 1.8 gather_fusion
  281.1 2.2 fusion
  283.2 1.0 reshape.101
  284.3 1.3 collective-permute-start
  285.6 1.3 collective-permute-start.1
  286.9 0.7 copy.36
  287.6 7.5 %all-to-all-start = ((bf16[16,32,128]{2,0,1:T(8,128)(2,1)}), bf16[16,32,128]{2,0,1:T(8,128)(2,1)S(1)}, u32[]{:S(2)}, u32[]{:S(2)}) async-start(bf16[16,32,128]{2,0,1:T(8,128)(2,1)} %copy.36), calls=%async_computation | async-start | bytes 262144 | tf_op jit(solution)/shard_map/all_to_all | solution.py:79
  295.1 1.0 copy.45
  296.1 9.6 %all-to-all-done = bf16[16,32,128]{2,0,1:T(8,128)(2,1)S(1)} async-done(((bf16[16,32,128]{2,0,1:T(8,128)(2,1)}), bf16[16,32,128]{2,0,1:T(8,128)(2,1)S(1)}, u32[]{:S(2)}, u32[]{:S(2)}) %all-to-all-start) | async-done | bytes 131104 | tf_op jit(solution)/shard_map/all_to_all | solution.py:79
  305.8 0.1 convert_element_type.48
  305.9 0.6 gather_fusion.1
  306.5 2.1 fusion.10
  308.6 0.1 copy.40
  308.7 0.7 broadcast_in_dim_reshape.7
  309.4 0.8 broadcast_in_dim_reshape.6
  (31 shorter events, 0.4 us)
Async XLA Ops:
  7.2 299.3 %copy-start = (bf16[1,8,384,384]{3,2,1,0:T(8,128)(2,1)S(1)}, bf16[1,8,384,384]{3,2,1,0:T(8,128)(2,1)}, u32[]{:S(2)}) copy-start(bf16[1,8,384,384]{3,2,1,0:T(8,128)(2,1)} %param.20) | copy-start | bytes 7077892
  7.2 5.2 %copy-start.2 = (f32[1,16,4352]{2,1,0:T(8,128)S(1)}, f32[1,16,4352]{2,1,0:T(8,128)}, u32[]{:S(2)}) copy-start(f32[1,16,4352]{2,1,0:T(8,128)} %param.13) | copy-start | bytes 835588
  7.2 5.2 %copy-start.4 = (s32[1,128]{1,0:T(1,128)S(1)}, s32[1,128]{1,0:T(1,128)}, u32[]{:S(2)}) copy-start(s32[1,128]{1,0:T(1,128)} %param.17) | copy-start | bytes 1540
  7.2 5.3 %copy-start.5 = (s32[1,8]{1,0:T(1,128)S(1)}, s32[1,8]{1,0:T(1,128)}, u32[]{:S(2)}) copy-start(s32[1,8]{1,0:T(1,128)} %param.18) | copy-start | bytes 100
  7.2 146.7 %all-reduce.3.cloned.1.call-start = ((), (), s32[]{:S(2)}) async-start(), calls=%async_computation.1 | async-start | bytes 131072 | tf_op jit(solution)/shard_map/psum | solution.py:59
  15.3 265.7 %copy-start.1 = (bf16[1,4352,128]{2,1,0:T(8,128)(2,1)S(1)}, bf16[1,4352,128]{2,1,0:T(8,128)(2,1)}, u32[]{:S(2)}) copy-start(bf16[1,4352,128]{2,1,0:T(8,128)(2,1)} %param.22) | copy-start | bytes 3342340
  230.1 3.3 %copy-start.3 = (f32[64,512]{1,0:T(8,128)S(1)}, f32[64,512]{1,0:T(8,128)}, u32[]{:S(2)}) copy-start(f32[64,512]{1,0:T(8,128)} %param.23) | copy-start | bytes 393220
  284.3 11.8 %collective-permute-start = (f32[16,1,128]{2,1,0:T(1,128)S(1)}, f32[16,1,128]{2,1,0:T(1,128)S(1)}, u32[]{:S(2)}, u32[]{:S(2)}) collective-permute-start(f32[16,1,128]{2,1,0:T(1,128)S(1)} %get-tuple-element.4), channel_id=1, source_target_pairs={{0,32},{32,64},{64,96},{96,128},{128,160},{160,192},{192,224},{1,3... | collective-permute-start | bytes 24584 | tf_op jit(solution)/shard_map/ppermute | solution.py:15
  285.6 10.5 %collective-permute-start.1 = (f32[16,1,128]{2,1,0:T(1,128)S(1)}, f32[16,1,128]{2,1,0:T(1,128)S(1)}, u32[]{:S(2)}, u32[]{:S(2)}) collective-permute-start(f32[16,1,128]{2,1,0:T(1,128)S(1)} %get-tuple-element.5), channel_id=1, source_target_pairs={{32,0},{64,32},{96,64},{128,96},{160,128},{192,160},{224,192},{33,... | collective-permute-start | bytes 24584 | tf_op jit(solution)/shard_map/ppermute | solution.py:17
  287.6 18.1 %all-to-all-start = ((bf16[16,32,128]{2,0,1:T(8,128)(2,1)}), bf16[16,32,128]{2,0,1:T(8,128)(2,1)S(1)}, u32[]{:S(2)}, u32[]{:S(2)}) async-start(bf16[16,32,128]{2,0,1:T(8,128)(2,1)} %copy.36), calls=%async_computation | async-start | bytes 262144 | tf_op jit(solution)/shard_map/all_to_all | solution.py:79
Sparse Core Ops, SparseCore 0:
  12.5 141.3 all-reduce.2
where the time goes:
time: 319 us; the launch traced here: 317 us
  waiting for transfers between devices  148 us (46%)
  blocking collectives  118 us (37%)
  matrix products  15 us (5%)
  between operations  14.3 us (4%)
  starting transfers between devices  10.1 us (3%)
  local copies, waits for them, and re-layouts  9.48 us (3%)
    psum x1, waiting for transfers between devices, shards(): level2 = lax.psum(contrib.astype(jnp.bfloat16), 'sub').astype(jnp.float32)  139 us
    psum x1, blocking collectives, shards(): level3 = lax.psum(top_term, ('group', 'sub'))  74.5 us
    all_gather x1, blocking collectives, shards(): lax.all_gather(coarse2_mine.astype(jnp.bfloat16), 'sub', axis=1, tiled=True)  43.7 us
    all_to_all x1, waiting for transfers between devices, shards(): lax.all_to_all(slots[:, :nsub, :].astype(jnp.bfloat16), 'sub', split_axis...  9.59 us
    all_to_all x1, starting transfers between devices, shards(): lax.all_to_all(slots[:, :nsub, :].astype(jnp.bfloat16), 'sub', split_axis...  7.46 us
  transfers between devices with their start and end apart: 4, of which 2 were waited for; matrix products, arithmetic and copies ran while one was open for 1% of the time, Pallas kernels for 0%

commit v1 on v0

v1 whole, which is shorter than its diff:
```python
import functools

import jax
import jax.numpy as jnp
from jax import lax
from jax.experimental import pallas as pl
from jax.experimental.pallas import tpu as pltpu
from jax.sharding import PartitionSpec as P

F32 = jnp.float32
BF16 = jnp.bfloat16
MESH = pl.DeviceIdType.MESH
NT = (((1,), (1,)), ((), ()))

NY, NZ = 4, 8


def dot(a, b):
    return jnp.dot(a, b, preferred_element_type=F32)


def dot_nt(a, b):
    return lax.dot_general(a, b, NT, preferred_element_type=F32)


def kernel(
    ngroup,
    nsub,
    resid_h,
    inner_h,
    weights_h,
    nbr_h,
    own_h,
    cidx_h,
    neumann_h,
    dirichlet_h,
    coupling_h,
    cb_h,
    basis_h,
    ginv_h,
    top_h,
    iface_h,
    inter_h,
    resid,
    inner,
    weights,
    nbr,
    cidx,
    neumann,
    dirichlet,
    coupling,
    cb,
    basis,
    ginv,
    top,
    scale,
    weighted,
    loc_all,
    own_all,
    bsend,
    bpk,
    bfull,
    ohl,
    hmask,
    lhs,
    lev,
    ohv,
    ginv_pad,
    nt_pad,
    p2,
    p3,
    c2,
    nsc,
    scaled,
    dsend,
    drecv,
    face,
    picked,
    iface,
    inter,
    in_sem,
    out_sem,
    send_sem,
    recv_sem,
):
    g = lax.axis_index("group")
    sub = lax.axis_index("sub")
    y, z = sub // NZ, sub % NZ
    par = sub % 2
    slots = nsub + 2
    kn = neumann.shape[0]
    ki = dirichlet.shape[0]
    bi = dirichlet.shape[1]

    loads = [
        (nbr_h, nbr),
        (weights_h, weights),
        (resid_h, resid),
        (cb_h, cb),
        (own_h, own_all.at[sub]),
        (basis_h, basis),
        (neumann_h, neumann),
        (top_h, top),
        (ginv_h, ginv),
        (cidx_h, cidx),
        (inner_h, inner),
        (coupling_h, coupling),
        (dirichlet_h, dirichlet),
    ]
    loads = [pltpu.make_async_copy(s, d, in_sem.at[i]) for i, (s, d) in enumerate(loads)]
    (ld_nbr, ld_w, ld_resid, ld_cb, ld_own, ld_basis, ld_neu, ld_top, ld_ginv, ld_cidx, ld_inner, ld_coup, ld_dir) = loads
    for ld in loads:
        ld.start()

    barrier = pltpu.get_barrier_semaphore()

    def greet_sub(o, _):
        pl.semaphore_signal(barrier, inc=1, device_id=(g, (sub + o) % nsub), device_id_type=MESH)
        return 0

    def greet_group(o, _):
        pl.semaphore_signal(barrier, inc=1, device_id=((g + o) % ngroup, sub), device_id_type=MESH)
        return 0

    lax.fori_loop(1, nsub, greet_sub, 0)
    lax.fori_loop(1, ngroup, greet_group, 0)

    def rcopy(src, dst, phase, tg, ts):
        return pltpu.make_async_remote_copy(
            src_ref=src,
            dst_ref=dst,
            send_sem=send_sem.at[phase],
            recv_sem=recv_sem.at[phase],
            device_id=(tg, ts),
            device_id_type=MESH,
        )

    def wait_recv(ref, phase):
        pltpu.make_async_copy(ref, ref, recv_sem.at[phase]).wait()

    def wait_send(ref, phase):
        pltpu.make_async_copy(ref, ref, send_sem.at[phase]).wait()

    def send_sub(buf, phase):
        def step(o, _):
            ts = ((y + o // NZ) % NY) * NZ + (z + o) % NZ
            rcopy(buf.at[sub], buf.at[sub], phase, g, ts).start()
            return 0

        lax.fori_loop(1, nsub, step, 0)

    lane = lax.broadcasted_iota(jnp.int32, (1, 128), 1)
    low = lane < 64
    ld_nbr.wait()
    ld_w.wait()
    ld_resid.wait()
    for j in range(slots):
        sl = pl.ds(128 * j, 128)
        sc = weights[:, sl]
        if j < nsub:
            sc = sc * nbr[0, j].astype(F32)
        scale[j] = sc
        weighted[:, sl] = (sc * resid[:, sl]).astype(BF16)
    ld_cb.wait()
    loc_all[sub] = dot(weighted[...], cb[...]).astype(BF16)

    ld_basis.wait()
    for k in range(NZ):
        t = pl.ds(128 * (k // 2), 128)
        a, b = basis[:32, t], basis[32:, t]
        if k % 2 == 0:
            pk = jnp.where(low, a, pltpu.roll(b, 64, 1))
        else:
            pk = jnp.where(low, pltpu.roll(a, 64, 1), b)
        bsend[k] = pk.astype(BF16)
    bpk[sub] = bsend[z]
    ld_own.wait()

    pl.semaphore_wait(barrier, nsub - 1 + ngroup - 1)

    send_sub(loc_all, 0)

    def send_z(o, _):
        tz = (z + o) % NZ
        rcopy(own_all.at[sub], own_all.at[sub], 1, g, y * NZ + tz).start()
        rcopy(bsend.at[tz], bpk.at[sub], 2, g, y * NZ + tz).start()
        return 0

    lax.fori_loop(1, NZ, send_z, 0)
    rows = pl.ds(pl.multiple_of(y * NZ, NZ), NZ)
    wait_recv(own_all.at[pl.ds(0, NZ - 1)], 1)
    wait_recv(bpk.at[pl.ds(0, NZ - 1)], 2)

    def send_y(o, _):
        ts = ((y + o) % NY) * NZ + z
        rcopy(own_all.at[rows], own_all.at[rows], 3, g, ts).start()
        rcopy(bpk.at[rows], bpk.at[rows], 4, g, ts).start()
        return 0

    lax.fori_loop(1, NY, send_y, 0)

    ld_top.wait()
    nt = dot(basis[...].astype(BF16), top[...].astype(BF16))
    mine_rows = pl.ds(pl.multiple_of(par * 64, 64), 64)
    other_rows = pl.ds(pl.multiple_of((1 - par) * 64, 64), 64)
    for k in range(NZ):
        v = nt[:, 128 * (k // 2) : 128 * (k // 2) + 128]
        if k % 2:
            v = pltpu.roll(v, 64, 1)
        nt_pad[mine_rows, pl.ds(128 * k, 128)] = jnp.where(low, v, 0.0).astype(BF16)
    nt_pad[other_rows, :] = jnp.zeros((64, 128 * NZ), BF16)
    ld_ginv.wait()
    ginv_pad[mine_rows, :] = ginv[...].astype(BF16)
    ginv_pad[other_rows, :] = jnp.zeros((64, ginv.shape[1]), BF16)

    wait_recv(own_all.at[pl.ds(0, nsub - NZ)], 3)

    def masks(s, _):
        o = own_all[s]
        lo, hi = o & 255, o >> 8
        ohl[:, pl.ds(pl.multiple_of(s * 128, 128), 128)] = (
            (lax.broadcasted_iota(jnp.int32, (256, 128), 0) == lo).astype(F32).astype(BF16)
        )
        for h in range(8):
            m = (hi == h).astype(F32)
            hmask[s, pl.ds(16 * h, 16), :] = jnp.broadcast_to(m, (16, 128)).astype(BF16)
        return 0

    lax.fori_loop(0, nsub, masks, 0)

    wait_recv(bpk.at[pl.ds(0, nsub - NZ)], 4)

    def unpack(q, _):
        p = bpk[q].astype(F32)
        at = pl.multiple_of(q * 64, 64)
        bfull[pl.ds(at, 32), :] = jnp.where(low, p, 0.0).astype(BF16)
        bfull[pl.ds(at + 32, 32), :] = jnp.where(low, pltpu.roll(p, 64, 1), 0.0).astype(BF16)
        return 0

    lax.fori_loop(0, nsub, unpack, 0)

    wait_recv(loc_all.at[pl.ds(0, nsub - 1)], 0)
    for s in range(nsub):
        v = loc_all[s]
        for h in range(8):
            lhs[pl.ds(16 * h, 16), pl.ds(128 * s, 128)] = v * hmask[s, pl.ds(16 * h, 16), :]
    level2 = dot_nt(lhs[...], ohl[...])
    for h in range(8):
        lev[:, pl.ds(256 * h, 256)] = level2[16 * h : 16 * h + 16, :].astype(BF16)
    p2[g] = dot(lev[...], bfull[...]).astype(BF16)

    def send_group(o, _):
        rcopy(p2.at[g], p2.at[g], 5, (g + o) % ngroup, sub).start()
        return 0

    lax.fori_loop(1, ngroup, send_group, 0)
    solved = dot_nt(lev[...], ginv_pad[...])
    wait_recv(p2.at[pl.ds(0, ngroup - 1)], 5)
    level3 = p2[0].astype(F32)
    for k in range(1, ngroup):
        level3 = level3 + p2[k].astype(F32)
    p3[z] = level3.astype(BF16)

    def send_top(o, _):
        rcopy(p3.at[z], p3.at[z], 6, g, y * NZ + (z + o) % NZ).start()
        return 0

    lax.fori_loop(1, NZ, send_top, 0)

    def pick(t, _):
        at = pl.multiple_of(t * 256, 256)
        ohv[pl.ds(at, 256), :] = (
            (lax.broadcasted_iota(jnp.int32, (256, 128), 0) + at == own_all[sub]).astype(F32).astype(BF16)
        )
        return 0

    lax.fori_loop(0, 8, pick, 0)

    wait_recv(p3.at[pl.ds(0, NZ - 1)], 6)
    lifted = dot_nt(jnp.concatenate([p3[k] for k in range(NZ)], axis=1), nt_pad[...])
    c2[sub] = (solved + lifted).astype(BF16)

    send_sub(c2, 7)
    ld_neu.wait()
    for k in range(kn):
        v = dot(weighted[:, 256 * k : 256 * k + 256], neumann[k])
        nsc[2 * k] = v[:, :128] * scale[2 * k]
        nsc[2 * k + 1] = v[:, 128:] * scale[2 * k + 1]
    wait_recv(c2.at[pl.ds(0, nsub - 1)], 7)
    coarse2 = jnp.concatenate([c2[2 * t] + c2[2 * t + 1] for t in range(nsub // 2)], axis=1)
    values = dot(coarse2, ohv[...]).astype(BF16)

    spread = dot_nt(values, cb[pl.ds(128 * nsub, 256), :])
    for i in range(2):
        scaled[nsub + i] = nsc[nsub + i] + scale[nsub + i] * spread[:, 128 * i : 128 * i + 128]

    to_upper = rcopy(scaled.at[nsub + 1], face.at[0], 8, jnp.minimum(g + 1, ngroup - 1), sub)
    to_lower = rcopy(scaled.at[nsub], face.at[1], 9, jnp.maximum(g - 1, 0), sub)

    @pl.when(g < ngroup - 1)
    def _():
        to_upper.start()

    @pl.when(g > 0)
    def _():
        to_lower.start()

    for c in range(NY):
        ty = (y + 1 + c) % NY
        first = ty * NZ
        spread = dot_nt(values, cb[pl.ds(pl.multiple_of(first * 128, 1024), 1024), :])
        for i in range(NZ):
            v = nsc[first + i] + scale[first + i] * spread[:, 128 * i : 128 * i + 128]
            scaled[first + i] = v
            dsend[first + i] = v.astype(BF16)

        def send_slot(o, _):
            to = first + (z + o) % NZ
            rcopy(dsend.at[to], drecv.at[sub], 10, g, to).start()
            return 0

        lax.fori_loop(0 if c < NY - 1 else 1, NZ, send_slot, 0)
    drecv[sub] = dsend[sub]

    @pl.when(g > 0)
    def _():
        to_upper.wait_recv()

    @pl.when(g == 0)
    def _():
        face[0] = jnp.zeros(face.shape[1:], F32)

    @pl.when(g < ngroup - 1)
    def _():
        to_lower.wait_recv()

    @pl.when(g == ngroup - 1)
    def _():
        face[1] = jnp.zeros(face.shape[1:], F32)

    ld_cidx.wait()
    ld_inner.wait()
    ld_coup.wait()
    ld_dir.wait()
    wait_recv(drecv.at[pl.ds(0, nsub - 1)], 10)
    for j in range(slots):
        got = drecv[j].astype(F32) if j < nsub else face[j - nsub]
        v = scaled[j] + got
        iface[:, pl.ds(128 * j, 128)] = v
        picked[j] = v.astype(BF16)
    st_iface = pltpu.make_async_copy(iface, iface_h, out_sem.at[0])
    st_iface.start()
    for k in range(ki):
        at = 2 * cidx[0, k]
        block = jnp.concatenate([picked[at], picked[at + 1]], axis=1)
        sl = pl.ds(bi * k, bi)
        rhs = (inner[:, sl] - dot(block, coupling[k])).astype(BF16)
        inter[:, sl] = dot(rhs, dirichlet[k])
    st_inter = pltpu.make_async_copy(inter, inter_h, out_sem.at[1])
    st_inter.start()

    wait_send(loc_all.at[pl.ds(0, nsub - 1)], 0)
    wait_send(own_all.at[pl.ds(0, NZ - 1)], 1)
    wait_send(bpk.at[pl.ds(0, NZ - 1)], 2)
    wait_send(own_all.at[pl.ds(0, nsub - NZ)], 3)
    wait_send(bpk.at[pl.ds(0, nsub - NZ)], 4)
    wait_send(p2.at[pl.ds(0, ngroup - 1)], 5)
    wait_send(p3.at[pl.ds(0, NZ - 1)], 6)
    wait_send(c2.at[pl.ds(0, nsub - 1)], 7)

    @pl.when(g < ngroup - 1)
    def _():
        to_upper.wait_send()

    @pl.when(g > 0)
    def _():
        to_lower.wait_send()

    wait_send(drecv.at[pl.ds(0, nsub - 1)], 10)
    st_iface.wait()
    st_inter.wait()


def shards(
    resid_iface,
    resid_inner,
    weights,
    nbr,
    own2,
    cidx,
    neumann,
    dirichlet,
    coupling,
    coarse_basis,
    group_basis,
    group_inverse,
    top_inverse,
):
    ngroup = lax.axis_size("group")
    nsub = lax.axis_size("sub")
    rows, width = resid_iface.shape[1:]
    inner_width = resid_inner.shape[2]
    group_width = group_inverse.shape[0]
    slots = nsub + 2
    ins = (
        resid_iface[0],
        resid_inner[0],
        weights,
        nbr,
        own2,
        cidx,
        neumann[0],
        dirichlet[0],
        coupling[0],
        coarse_basis[0],
        group_basis,
        group_inverse.T,
        top_inverse,
    )
    v, s = pltpu.VMEM, pltpu.SMEM
    staged = [
        (v if i not in (3, 5) else s)(a.shape, a.dtype) for i, a in enumerate(ins) if i != 4
    ]
    work = [
        v((slots, 1, 128), F32),
        v((rows, width), BF16),
        v((nsub, rows, 128), BF16),
        v((nsub, 1, 128), jnp.int32),
        v((NZ, 32, 128), BF16),
        v((nsub, 32, 128), BF16),
        v((group_width, 128), BF16),
        v((256, 128 * nsub), BF16),
        v((nsub, 128, 128), BF16),
        v((128, 128 * nsub), BF16),
        v((rows, group_width), BF16),
        v((group_width, 128), BF16),
        v((128, group_width), BF16),
        v((128, 128 * NZ), BF16),
        v((ngroup, rows, 128), BF16),
        v((NZ, rows, 128), BF16),
        v((nsub, rows, 128), BF16),
        v((slots, rows, 128), F32),
        v((slots, rows, 128), F32),
        v((nsub, rows, 128), BF16),
        v((nsub, rows, 128), BF16),
        v((2, rows, 128), F32),
        v((slots, rows, 128), BF16),
        v((rows, width), F32),
        v((rows, inner_width), F32),
    ]
    sems = [
        pltpu.SemaphoreType.DMA((13,)),
        pltpu.SemaphoreType.DMA((2,)),
        pltpu.SemaphoreType.DMA((11,)),
        pltpu.SemaphoreType.DMA((11,)),
    ]
    anywhere = pl.BlockSpec(memory_space=pl.ANY)
    iface, inter = pl.pallas_call(
        functools.partial(kernel, ngroup, nsub),
        out_shape=(
            jax.ShapeDtypeStruct((rows, width), F32),
            jax.ShapeDtypeStruct((rows, inner_width), F32),
        ),
        in_specs=[anywhere] * len(ins),
        out_specs=(anywhere, anywhere),
        scratch_shapes=staged + work + sems,
        compiler_params=pltpu.CompilerParams(
            collective_id=0, has_side_effects=True, vmem_limit_bytes=56 * 2**20
        ),
        name="bddc",
    )(*ins)
    return iface[None], inter[None]


def solution(mesh):
    one = P(("group", "sub"), None)
    two = P(("group", "sub"), None, None)
    three = P(("group", "sub"), None, None, None)
    return jax.shard_map(
        shards,
        mesh=mesh,
        in_specs=(two, two, one, one, one, one, three, three, three, two, one, P("group", "sub"), P()),
        out_specs=(two, two),
        check_vma=False,
    )
```

time: 319 us -> 55.3 us (0.17)
  waiting for transfers between devices: 148 us -> 0 us
  blocking collectives: 118 us -> 0 us
  Pallas kernels: 0 us -> 50.6 us
  matrix products: 15 us -> 0 us
  between operations: 14.3 us -> 0.64 us
  starting transfers between devices: 10.1 us -> 0 us
  local copies, waits for them, and re-layouts: 9.48 us -> 3.3 us
    psum x1 -> x0, waiting for transfers between devices: 139 us -> none  [shards(): level2 = lax.psum(contrib.astype(jnp.bfloat16), 'sub').astype(jnp.float32)]
    psum x1 -> x0, blocking collectives: 74.5 us -> none  [shards(): level3 = lax.psum(top_term, ('group', 'sub'))]
    pallas_call x0 -> x1, Pallas kernels: none -> 50.6 us  [shards(): pl.pallas_call(functools.partial(kernel, ngroup, nsub), out_shape=(jax.Sh...]
    all_gather x1 -> x0, blocking collectives: 43.7 us -> none  [shards(): lax.all_gather(coarse2_mine.astype(jnp.bfloat16), 'sub', axis=1, tiled=True)]
    dot_general x9 -> x0, matrix products: 15 us -> none  [the longest x1 2.19 us: shards(): lax.dot_general(values, coarse_basis[0], (((1,), (1,)), ((), ())), prefer...]
    all_to_all x1 -> x0, waiting for transfers between devices: 9.59 us -> none  [shards(): lax.all_to_all(slots[:, :nsub, :].astype(jnp.bfloat16), 'sub', split_axis...]
    all_to_all x1 -> x0, starting transfers between devices: 7.46 us -> none  [shards(): lax.all_to_all(slots[:, :nsub, :].astype(jnp.bfloat16), 'sub', split_axis...]
  transfers between devices with their start and end apart: 4 -> 0, of which waited for: 2 -> 0; matrix products, arithmetic and copies ran while one was open for 1% -> 0% of each run, Pallas kernels for 0% -> 0%
where the time goes in v1:
time: 55.3 us; the launch traced here: 54.5 us
  Pallas kernels  50.6 us (92%)
  local copies, waits for them, and re-layouts  3.3 us (6%)
  between operations  0.64 us (1%)
    pallas_call x1, Pallas kernels, shards(): pl.pallas_call(functools.partial(kernel, ngroup, nsub), out_shape=(jax.Sh...  50.6 us
    unnamed x2, local copies, waits for them, and re-layouts  3.3 us

profile of v1, /device:TPU:32, one launch (start us, length us, event | category | flops | bytes accessed | tf_op | source)
XLA Modules:
  0.0 54.5 jit_solution(11837106112683681537)
XLA Ops:
  0.6 50.6 %bddc.1 = (f32[16,4352]{1,0:T(8,128)}, f32[16,3072]{1,0:T(8,128)}) custom-call(f32[16,4352]{1,0:T(8,128)} %bitcast.14, f32[16,3072]{1,0:T(8,128)} %bitcast.17, f32[1,4352]{1,0:T(1,128)} %weights_h.1, s32[1,32]{1,0:T(1,128)} %nbr_h.1, s32[1,128]{1,0:T(1,128)} %own_h.1, s32[1,8]{1,0:T(1,128)} %cidx_h.1, bf16[17,256,256]{2,1,0:T(8,128)(2,1)} %bitcast.10, ...), custom_call_target="tpu_custom_call" | custom-call | tf_op jit(solution)/shard_map/bddc/pallas_call | solution.py:458
  51.2 1.7 %copy.17 = f32[1,16,4352]{2,1,0:T(8,128)} copy(f32[1,16,4352]{2,1,0:T(8,128)} %bitcast.15) | data formatting | bytes 557056
  52.9 1.6 %copy.18 = f32[1,16,3072]{2,1,0:T(8,128)} copy(f32[1,16,3072]{2,1,0:T(8,128)} %bitcast.16) | data formatting | bytes 393216

commit v2 on v1

--- a/solution.py
+++ b/solution.py
@@ -39,8 +39,8 @@
     basis_h,
     ginv_h,
     top_h,
-    iface_h,
-    inter_h,
+    iface,
+    inter,
     resid,
     inner,
     weights,
@@ -66,7 +66,9 @@
     lev,
     ohv,
     ginv_pad,
-    nt_pad,
+    nsend,
+    npk,
+    nz,
     p2,
     p3,
     c2,
@@ -76,10 +78,8 @@
     drecv,
     face,
     picked,
-    iface,
-    inter,
+    quick,
     in_sem,
-    out_sem,
     send_sem,
     recv_sem,
 ):
@@ -109,7 +109,7 @@
     ]
     loads = [pltpu.make_async_copy(s, d, in_sem.at[i]) for i, (s, d) in enumerate(loads)]
     (ld_nbr, ld_w, ld_resid, ld_cb, ld_own, ld_basis, ld_neu, ld_top, ld_ginv, ld_cidx, ld_inner, ld_coup, ld_dir) = loads
-    for ld in loads:
+    for ld in (ld_nbr, ld_w, ld_resid, ld_cb, ld_basis, ld_own):
         ld.start()
 
     barrier = pltpu.get_barrier_semaphore()
@@ -141,16 +141,42 @@
     def wait_send(ref, phase):
         pltpu.make_async_copy(ref, ref, send_sem.at[phase]).wait()
 
-    def send_sub(buf, phase):
-        def step(o, _):
-            ts = ((y + o // NZ) % NY) * NZ + (z + o) % NZ
-            rcopy(buf.at[sub], buf.at[sub], phase, g, ts).start()
-            return 0
-
-        lax.fori_loop(1, nsub, step, 0)
+    def far_first(i, n):
+        return n // 2 + jnp.where(i % 2 == 1, -((i + 1) // 2), i // 2)
 
     lane = lax.broadcasted_iota(jnp.int32, (1, 128), 1)
     low = lane < 64
+    def pack_z(src, dst):
+        for k in range(NZ):
+            t = slice(128 * (k // 2), 128 * (k // 2) + 128)
+            a, b = src[:32, t], src[32:, t]
+            if k % 2 == 0:
+                pk = jnp.where(low, a, pltpu.roll(b, 64, 1))
+            else:
+                pk = jnp.where(low, pltpu.roll(a, 64, 1), b)
+            dst[k] = pk.astype(BF16)
+
+    def unpack(src, dst, q):
+        p = src[q].astype(F32)
+        at = q * 64 if isinstance(q, int) else pl.multiple_of(q * 64, 64)
+        dst[pl.ds(at, 32), :] = jnp.where(low, p, 0.0).astype(BF16)
+        dst[pl.ds(at + 32, 32), :] = jnp.where(low, pltpu.roll(p, 64, 1), 0.0).astype(BF16)
+
+    ld_basis.wait()
+    pack_z(basis[...], bsend)
+    bpk[sub] = bsend[z]
+    ld_own.wait()
+
+    pl.semaphore_wait(barrier, nsub - 1 + ngroup - 1)
+
+    def send_z(i, _):
+        tz = (z + far_first(i, NZ)) % NZ
+        rcopy(own_all.at[sub], own_all.at[sub], 1, g, y * NZ + tz).start()
+        rcopy(bsend.at[tz], bpk.at[sub], 2, g, y * NZ + tz).start()
+        return 0
+
+    lax.fori_loop(0, NZ - 1, send_z, 0)
+
     ld_nbr.wait()
     ld_w.wait()
     ld_resid.wait()
@@ -164,54 +190,56 @@
     ld_cb.wait()
     loc_all[sub] = dot(weighted[...], cb[...]).astype(BF16)
 
-    ld_basis.wait()
-    for k in range(NZ):
-        t = pl.ds(128 * (k // 2), 128)
-        a, b = basis[:32, t], basis[32:, t]
-        if k % 2 == 0:
-            pk = jnp.where(low, a, pltpu.roll(b, 64, 1))
-        else:
-            pk = jnp.where(low, pltpu.roll(a, 64, 1), b)
-        bsend[k] = pk.astype(BF16)
-    bpk[sub] = bsend[z]
-    ld_own.wait()
-
-    pl.semaphore_wait(barrier, nsub - 1 + ngroup - 1)
-
-    send_sub(loc_all, 0)
-
-    def send_z(o, _):
-        tz = (z + o) % NZ
-        rcopy(own_all.at[sub], own_all.at[sub], 1, g, y * NZ + tz).start()
-        rcopy(bsend.at[tz], bpk.at[sub], 2, g, y * NZ + tz).start()
-        return 0
-
-    lax.fori_loop(1, NZ, send_z, 0)
-    rows = pl.ds(pl.multiple_of(y * NZ, NZ), NZ)
-    wait_recv(own_all.at[pl.ds(0, NZ - 1)], 1)
-    wait_recv(bpk.at[pl.ds(0, NZ - 1)], 2)
-
-    def send_y(o, _):
-        ts = ((y + o) % NY) * NZ + z
-        rcopy(own_all.at[rows], own_all.at[rows], 3, g, ts).start()
-        rcopy(bpk.at[rows], bpk.at[rows], 4, g, ts).start()
-        return 0
-
-    lax.fori_loop(1, NY, send_y, 0)
+    def send_loc(o, _):
+        ts = ((y + far_first(o % NY, NY)) % NY) * NZ + (z + far_first(o // NY, NZ)) % NZ
+        rcopy(loc_all.at[sub], loc_all.at[sub], 0, g, ts).start()
+        return 0
+
+    lax.fori_loop(0, nsub - 1, send_loc, 0)
+    for ld in (ld_top, ld_ginv, ld_coup, ld_dir, ld_inner, ld_neu, ld_cidx):
+        ld.start()
 
     ld_top.wait()
-    nt = dot(basis[...].astype(BF16), top[...].astype(BF16))
+    pack_z(dot(basis[...].astype(BF16), top[...].astype(BF16)), nsend)
+    npk[z] = nsend[z]
+
+    def send_n(i, _):
+        tz = (z + far_first(i, NZ)) % NZ
+        rcopy(nsend.at[tz], npk.at[z], 11, g, y * NZ + tz).start()
+        return 0
+
+    lax.fori_loop(0, NZ - 1, send_n, 0)
     mine_rows = pl.ds(pl.multiple_of(par * 64, 64), 64)
     other_rows = pl.ds(pl.multiple_of((1 - par) * 64, 64), 64)
-    for k in range(NZ):
-        v = nt[:, 128 * (k // 2) : 128 * (k // 2) + 128]
-        if k % 2:
-            v = pltpu.roll(v, 64, 1)
-        nt_pad[mine_rows, pl.ds(128 * k, 128)] = jnp.where(low, v, 0.0).astype(BF16)
-    nt_pad[other_rows, :] = jnp.zeros((64, 128 * NZ), BF16)
     ld_ginv.wait()
     ginv_pad[mine_rows, :] = ginv[...].astype(BF16)
     ginv_pad[other_rows, :] = jnp.zeros((64, ginv.shape[1]), BF16)
+
+    rows = pl.ds(pl.multiple_of(y * NZ, NZ), NZ)
+    wait_recv(own_all.at[pl.ds(0, NZ - 1)], 1)
+
+    def send_own_y(i, _):
+        ts = ((y + far_first(i, NY)) % NY) * NZ + z
+        rcopy(own_all.at[rows], own_all.at[rows], 3, g, ts).start()
+        return 0
+
+    lax.fori_loop(0, NY - 1, send_own_y, 0)
+    wait_recv(bpk.at[pl.ds(0, NZ - 1)], 2)
+
+    def send_basis_y(i, _):
+        ts = ((y + far_first(i, NY)) % NY) * NZ + z
+        rcopy(bpk.at[rows], bpk.at[rows], 4, g, ts).start()
+        return 0
+
+    lax.fori_loop(0, NY - 1, send_basis_y, 0)
+
+    ld_coup.wait()
+    ld_dir.wait()
+    ld_inner.wait()
+    for k in range(ki):
+        sl = pl.ds(bi * k, bi)
+        quick[k] = dot(coupling[k], dirichlet[k]).astype(BF16)
+        inter[:, sl] = dot(inner[:, sl].astype(BF16), dirichlet[k])
 
     wait_recv(own_all.at[pl.ds(0, nsub - NZ)], 3)
 
@@ -230,14 +258,11 @@
 
     wait_recv(bpk.at[pl.ds(0, nsub - NZ)], 4)
 
-    def unpack(q, _):
-        p = bpk[q].astype(F32)
-        at = pl.multiple_of(q * 64, 64)
-        bfull[pl.ds(at, 32), :] = jnp.where(low, p, 0.0).astype(BF16)
-        bfull[pl.ds(at + 32, 32), :] = jnp.where(low, pltpu.roll(p, 64, 1), 0.0).astype(BF16)
-        return 0
-
-    lax.fori_loop(0, nsub, unpack, 0)
+    def unpack_basis(q, _):
+        unpack(bpk, bfull, q)
+        return 0
+
+    lax.fori_loop(0, nsub, unpack_basis, 0)
 
     wait_recv(loc_all.at[pl.ds(0, nsub - 1)], 0)
     for s in range(nsub):
@@ -255,17 +280,24 @@
 
     lax.fori_loop(1, ngroup, send_group, 0)
     solved = dot_nt(lev[...], ginv_pad[...])
+    wait_recv(npk.at[pl.ds(0, NZ - 1)], 11)
+    for k in range(NZ):
+        unpack(npk, nz, k)
     wait_recv(p2.at[pl.ds(0, ngroup - 1)], 5)
     level3 = p2[0].astype(F32)
     for k in range(1, ngroup):
         level3 = level3 + p2[k].astype(F32)
-    p3[z] = level3.astype(BF16)
-
-    def send_top(o, _):
-        rcopy(p3.at[z], p3.at[z], 6, g, y * NZ + (z + o) % NZ).start()
-        return 0
-
-    lax.fori_loop(1, NZ, send_top, 0)
+
+    part = dot_nt(level3.astype(BF16), nz[...])
+    for t in range(NZ // 2):
+        own_part = jnp.where(z // 2 == t, solved, 0.0)
+        p3[z, pl.ds(16 * t, 16), :] = (part[:, 128 * t : 128 * t + 128] + own_part).astype(BF16)
+
+    def send_part(i, _):
+        rcopy(p3.at[z], p3.at[z], 6, g, y * NZ + (z + far_first(i, NZ)) % NZ).start()
+        return 0
+
+    lax.fori_loop(0, NZ - 1, send_part, 0)
 
     def pick(t, _):
         at = pl.multiple_of(t * 256, 256)
@@ -275,19 +307,26 @@
         return 0
 
     lax.fori_loop(0, 8, pick, 0)
-
-    wait_recv(p3.at[pl.ds(0, NZ - 1)], 6)
-    lifted = dot_nt(jnp.concatenate([p3[k] for k in range(NZ)], axis=1), nt_pad[...])
-    c2[sub] = (solved + lifted).astype(BF16)
-
-    send_sub(c2, 7)
     ld_neu.wait()
     for k in range(kn):
         v = dot(weighted[:, 256 * k : 256 * k + 256], neumann[k])
         nsc[2 * k] = v[:, :128] * scale[2 * k]
         nsc[2 * k + 1] = v[:, 128:] * scale[2 * k + 1]
-    wait_recv(c2.at[pl.ds(0, nsub - 1)], 7)
-    coarse2 = jnp.concatenate([c2[2 * t] + c2[2 * t + 1] for t in range(nsub // 2)], axis=1)
+    wait_recv(p3.at[pl.ds(0, NZ - 1)], 6)
+    c2y = p3[0].astype(F32)
+    for k in range(1, NZ):
+        c2y = c2y + p3[k].astype(F32)
+    c2[y] = c2y.astype(BF16)
+
+    def send_coarse(i, _):
+        rcopy(c2.at[y], c2.at[y], 7, g, ((y + far_first(i, NY)) % NY) * NZ + z).start()
+        return 0
+
+    lax.fori_loop(0, NY - 1, send_coarse, 0)
+    wait_recv(c2.at[pl.ds(0, NY - 1)], 7)
+    coarse2 = jnp.concatenate(
+        [c2[k, 16 * t : 16 * t + 16, :] for k in range(NY) for t in range(NZ // 2)], axis=1
+    )
     values = dot(coarse2, ohv[...]).astype(BF16)
 
     spread = dot_nt(values, cb[pl.ds(128 * nsub, 256), :])
@@ -306,7 +345,7 @@
         to_lower.start()
 
     for c in range(NY):
-        ty = (y + 1 + c) % NY
+        ty = (y + (2, 1, 3, 0)[c]) % NY
         first = ty * NZ
         spread = dot_nt(values, cb[pl.ds(pl.multiple_of(first * 128, 1024), 1024), :])
         for i in range(NZ):
@@ -315,11 +354,11 @@
             dsend[first + i] = v.astype(BF16)
 
         def send_slot(o, _):
-            to = first + (z + o) % NZ
+            to = first + (z + far_first(o, NZ)) % NZ
             rcopy(dsend.at[to], drecv.at[sub], 10, g, to).start()
             return 0
 
-        lax.fori_loop(0 if c < NY - 1 else 1, NZ, send_slot, 0)
+        lax.fori_loop(0, NZ if c < NY - 1 else NZ - 1, send_slot, 0)
     drecv[sub] = dsend[sub]
 
     @pl.when(g > 0)
@@ -339,25 +378,17 @@
         face[1] = jnp.zeros(face.shape[1:], F32)
 
     ld_cidx.wait()
-    ld_inner.wait()
-    ld_coup.wait()
-    ld_dir.wait()
     wait_recv(drecv.at[pl.ds(0, nsub - 1)], 10)
     for j in range(slots):
         got = drecv[j].astype(F32) if j < nsub else face[j - nsub]
         v = scaled[j] + got
         iface[:, pl.ds(128 * j, 128)] = v
         picked[j] = v.astype(BF16)
-    st_iface = pltpu.make_async_copy(iface, iface_h, out_sem.at[0])
-    st_iface.start()
     for k in range(ki):
         at = 2 * cidx[0, k]
         block = jnp.concatenate([picked[at], picked[at + 1]], axis=1)
         sl = pl.ds(bi * k, bi)
-        rhs = (inner[:, sl] - dot(block, coupling[k])).astype(BF16)
-        inter[:, sl] = dot(rhs, dirichlet[k])
-    st_inter = pltpu.make_async_copy(inter, inter_h, out_sem.at[1])
-    st_inter.start()
+        inter[:, sl] = inter[:, sl] - dot(block, quick[k])
 
     wait_send(loc_all.at[pl.ds(0, nsub - 1)], 0)
     wait_send(own_all.at[pl.ds(0, NZ - 1)], 1)
@@ -366,7 +397,8 @@
     wait_send(bpk.at[pl.ds(0, nsub - NZ)], 4)
     wait_send(p2.at[pl.ds(0, ngroup - 1)], 5)
     wait_send(p3.at[pl.ds(0, NZ - 1)], 6)
-    wait_send(c2.at[pl.ds(0, nsub - 1)], 7)
+    wait_send(c2.at[pl.ds(0, NY - 1)], 7)
+    wait_send(npk.at[pl.ds(0, NZ - 1)], 11)
 
     @pl.when(g < ngroup - 1)
     def _():
@@ -377,8 +409,6 @@
         to_lower.wait_send()
 
     wait_send(drecv.at[pl.ds(0, nsub - 1)], 10)
-    st_iface.wait()
-    st_inter.wait()
 
 
 def shards(
@@ -435,37 +465,37 @@
         v((rows, group_width), BF16),
         v((group_width, 128), BF16),
         v((128, group_width), BF16),
-        v((128, 128 * NZ), BF16),
+        v((NZ, 32, 128), BF16),
+        v((NZ, 32, 128), BF16),
+        v((64 * NZ, 128), BF16),
         v((ngroup, rows, 128), BF16),
-        v((NZ, rows, 128), BF16),
-        v((nsub, rows, 128), BF16),
+        v((NZ, rows * NZ // 2, 128), BF16),
+        v((NY, rows * NZ // 2, 128), BF16),
         v((slots, rows, 128), F32),
         v((slots, rows, 128), F32),
         v((nsub, rows, 128), BF16),
         v((nsub, rows, 128), BF16),
         v((2, rows, 128), F32),
         v((slots, rows, 128), BF16),
-        v((rows, width), F32),
-        v((rows, inner_width), F32),
+        v(coupling.shape[1:], BF16),
     ]
     sems = [
         pltpu.SemaphoreType.DMA((13,)),
-        pltpu.SemaphoreType.DMA((2,)),
-        pltpu.SemaphoreType.DMA((11,)),
-        pltpu.SemaphoreType.DMA((11,)),
+        pltpu.SemaphoreType.DMA((12,)),
+        pltpu.SemaphoreType.DMA((12,)),
     ]
     anywhere = pl.BlockSpec(memory_space=pl.ANY)
     iface, inter = pl.pallas_call(
         functools.partial(kernel, ngroup, nsub),
         out_shape=(
-            jax.ShapeDtypeStruct((rows, width), F32),
-            jax.ShapeDtypeStruct((rows, inner_width), F32),
+            pltpu.VMEM((rows, width), F32),
+            pltpu.VMEM((rows, inner_width), F32),
         ),
         in_specs=[anywhere] * len(ins),
-        out_specs=(anywhere, anywhere),
+        out_specs=(pl.BlockSpec(memory_space=pltpu.VMEM),) * 2,
         scratch_shapes=staged + work + sems,
         compiler_params=pltpu.CompilerParams(
-            collective_id=0, has_side_effects=True, vmem_limit_bytes=56 * 2**20
+            collective_id=0, has_side_effects=True, vmem_limit_bytes=60 * 2**20
         ),
         name="bddc",
     )(*ins)

time: 55.3 us -> 45.7 us (0.83); the launches traced: 54.5 us -> 45.6 us
  Pallas kernels: 50.6 us -> 43.5 us
  local copies, waits for them, and re-layouts: 3.3 us -> 1.39 us
    pallas_call x1, Pallas kernels: 50.6 us -> 43.5 us  [shards(): pl.pallas_call(functools.partial(kernel, ngroup, nsub), out_shape=(pltpu....]
    unnamed x2, local copies, waits for them, and re-layouts: 3.3 us -> 1.39 us
where the time goes in v2:
time: 45.7 us; the launch traced here: 45.6 us
  Pallas kernels  43.5 us (95%)
  local copies, waits for them, and re-layouts  1.39 us (3%)
  between operations  0.64 us (1%)
    pallas_call x1, Pallas kernels, shards(): pl.pallas_call(functools.partial(kernel, ngroup, nsub), out_shape=(pltpu....  43.5 us
    unnamed x2, local copies, waits for them, and re-layouts  1.39 us

profile of v2, /device:TPU:32, one launch (start us, length us, event | category | flops | bytes accessed | tf_op | source)
XLA Modules:
  0.0 45.6 jit_solution(11298590824940696319)
XLA Ops:
  0.6 43.5 %bddc.1 = (f32[16,4352]{1,0:T(8,128)S(1)}, f32[16,3072]{1,0:T(8,128)S(1)}) custom-call(f32[16,4352]{1,0:T(8,128)} %bitcast.16, f32[16,3072]{1,0:T(8,128)} %bitcast.17, f32[1,4352]{1,0:T(1,128)} %weights_h.1, s32[1,32]{1,0:T(1,128)} %nbr_h.1, s32[1,128]{1,0:T(1,128)} %own_h.1, s32[1,8]{1,0:T(1,128)} %cidx_h.1, bf16[17,256,256]{2,1,0:T(8,128)(2,1)} %bitcast.12, ...), custom_call_target="tpu_custom_call" | custom-call | tf_op jit(solution)/shard_map/bddc/pallas_call | solution.py:488
  44.2 0.7 %copy.17 = f32[1,16,4352]{2,1,0:T(8,128)} copy(f32[1,16,4352]{2,1,0:T(8,128)S(1)} %bitcast.9) | data formatting | bytes 557056
  44.9 0.7 %copy.18 = f32[1,16,3072]{2,1,0:T(8,128)} copy(f32[1,16,3072]{2,1,0:T(8,128)S(1)} %bitcast.10) | data formatting | bytes 393216

commit v3 on v2

--- a/solution.py
+++ b/solution.py
@@ -61,8 +61,9 @@
     bpk,
     bfull,
     ohl,
-    hmask,
     lhs,
+    lev_send,
+    lev_recv,
     lev,
     ohv,
     ginv_pad,
@@ -97,7 +98,7 @@
         (weights_h, weights),
         (resid_h, resid),
         (cb_h, cb),
-        (own_h, own_all.at[sub]),
+        (own_h, own_all.at[z]),
         (basis_h, basis),
         (neumann_h, neumann),
         (top_h, top),
@@ -109,21 +110,35 @@
     ]
     loads = [pltpu.make_async_copy(s, d, in_sem.at[i]) for i, (s, d) in enumerate(loads)]
     (ld_nbr, ld_w, ld_resid, ld_cb, ld_own, ld_basis, ld_neu, ld_top, ld_ginv, ld_cidx, ld_inner, ld_coup, ld_dir) = loads
-    for ld in (ld_nbr, ld_w, ld_resid, ld_cb, ld_basis, ld_own):
+    for ld in (ld_cb, ld_resid, ld_nbr, ld_w, ld_basis, ld_own):
         ld.start()
 
+    def far_first(i, n):
+        return n // 2 + jnp.where(i % 2 == 1, -((i + 1) // 2), i // 2)
+
+    def z_at(i):
+        return (z + far_first(i, NZ)) % NZ
+
+    def y_at(i):
+        return (y + far_first(i, NY)) % NY
+
+    def plane_peer(o):
+        tg = (g // 2 + far_first(o // (2 * NY), ngroup // 2)) % (ngroup // 2) * 2 + (g + 1 - o % 2) % 2
+        return tg, y_at(o // 2 % NY) * NZ + z
+
     barrier = pltpu.get_barrier_semaphore()
-
-    def greet_sub(o, _):
-        pl.semaphore_signal(barrier, inc=1, device_id=(g, (sub + o) % nsub), device_id_type=MESH)
-        return 0
-
-    def greet_group(o, _):
-        pl.semaphore_signal(barrier, inc=1, device_id=((g + o) % ngroup, sub), device_id_type=MESH)
-        return 0
-
-    lax.fori_loop(1, nsub, greet_sub, 0)
-    lax.fori_loop(1, ngroup, greet_group, 0)
+    plane = ngroup * NY
+
+    def greet_z(i, _):
+        pl.semaphore_signal(barrier, inc=1, device_id=(g, y * NZ + z_at(i)), device_id_type=MESH)
+        return 0
+
+    def greet_plane(o, _):
+        pl.semaphore_signal(barrier, inc=1, device_id=plane_peer(o), device_id_type=MESH)
+        return 0
+
+    lax.fori_loop(0, NZ - 1, greet_z, 0)
+    lax.fori_loop(0, plane - 1, greet_plane, 0)
 
     def rcopy(src, dst, phase, tg, ts):
         return pltpu.make_async_remote_copy(
@@ -140,9 +155,6 @@
 
     def wait_send(ref, phase):
         pltpu.make_async_copy(ref, ref, send_sem.at[phase]).wait()
-
-    def far_first(i, n):
-        return n // 2 + jnp.where(i % 2 == 1, -((i + 1) // 2), i // 2)
 
     lane = lax.broadcasted_iota(jnp.int32, (1, 128), 1)
     low = lane < 64
@@ -162,21 +174,6 @@
         dst[pl.ds(at, 32), :] = jnp.where(low, p, 0.0).astype(BF16)
         dst[pl.ds(at + 32, 32), :] = jnp.where(low, pltpu.roll(p, 64, 1), 0.0).astype(BF16)
 
-    ld_basis.wait()
-    pack_z(basis[...], bsend)
-    bpk[sub] = bsend[z]
-    ld_own.wait()
-
-    pl.semaphore_wait(barrier, nsub - 1 + ngroup - 1)
-
-    def send_z(i, _):
-        tz = (z + far_first(i, NZ)) % NZ
-        rcopy(own_all.at[sub], own_all.at[sub], 1, g, y * NZ + tz).start()
-        rcopy(bsend.at[tz], bpk.at[sub], 2, g, y * NZ + tz).start()
-        return 0
-
-    lax.fori_loop(0, NZ - 1, send_z, 0)
-
     ld_nbr.wait()
     ld_w.wait()
     ld_resid.wait()
@@ -188,51 +185,94 @@
         scale[j] = sc
         weighted[:, sl] = (sc * resid[:, sl]).astype(BF16)
     ld_cb.wait()
-    loc_all[sub] = dot(weighted[...], cb[...]).astype(BF16)
-
-    def send_loc(o, _):
-        ts = ((y + far_first(o % NY, NY)) % NY) * NZ + (z + far_first(o // NY, NZ)) % NZ
-        rcopy(loc_all.at[sub], loc_all.at[sub], 0, g, ts).start()
-        return 0
-
-    lax.fori_loop(0, nsub - 1, send_loc, 0)
-    for ld in (ld_top, ld_ginv, ld_coup, ld_dir, ld_inner, ld_neu, ld_cidx):
+    loc_all[z] = dot(weighted[...], cb[...]).astype(BF16)
+    ld_basis.wait()
+    pack_z(basis[...], bsend)
+    bpk[z] = bsend[z]
+    ld_own.wait()
+
+    for ld in (ld_top, ld_ginv, ld_neu, ld_coup, ld_dir, ld_inner, ld_cidx):
         ld.start()
+
+    pl.semaphore_wait(barrier, NZ - 1 + plane - 1)
+
+    def send_loc(i, _):
+        tz = z_at(i)
+        rcopy(own_all.at[z], own_all.at[z], 1, g, y * NZ + tz).start()
+        rcopy(loc_all.at[z], loc_all.at[z], 0, g, y * NZ + tz).start()
+        return 0
+
+    lax.fori_loop(0, NZ - 1, send_loc, 0)
+
+    def send_z(i, _):
+        tz = z_at(i)
+        rcopy(bsend.at[tz], bpk.at[z], 2, g, y * NZ + tz).start()
+        return 0
+
+    lax.fori_loop(0, NZ - 1, send_z, 0)
 
     ld_top.wait()
     pack_z(dot(basis[...].astype(BF16), top[...].astype(BF16)), nsend)
     npk[z] = nsend[z]
-
-    def send_n(i, _):
-        tz = (z + far_first(i, NZ)) % NZ
-        rcopy(nsend.at[tz], npk.at[z], 11, g, y * NZ + tz).start()
-        return 0
-
-    lax.fori_loop(0, NZ - 1, send_n, 0)
     mine_rows = pl.ds(pl.multiple_of(par * 64, 64), 64)
     other_rows = pl.ds(pl.multiple_of((1 - par) * 64, 64), 64)
     ld_ginv.wait()
     ginv_pad[mine_rows, :] = ginv[...].astype(BF16)
     ginv_pad[other_rows, :] = jnp.zeros((64, ginv.shape[1]), BF16)
 
-    rows = pl.ds(pl.multiple_of(y * NZ, NZ), NZ)
     wait_recv(own_all.at[pl.ds(0, NZ - 1)], 1)
-
-    def send_own_y(i, _):
-        ts = ((y + far_first(i, NY)) % NY) * NZ + z
-        rcopy(own_all.at[rows], own_all.at[rows], 3, g, ts).start()
-        return 0
-
-    lax.fori_loop(0, NY - 1, send_own_y, 0)
+    wait_recv(loc_all.at[pl.ds(0, NZ - 1)], 0)
+    count = lax.broadcasted_iota(jnp.int32, (256, 128), 0).astype(F32).astype(BF16)
+    one, nil = jnp.ones((256, 128), BF16), jnp.zeros((256, 128), BF16)
+    for s in range(NZ):
+        at = pl.ds(128 * s, 128)
+        o = own_all[s]
+        lo = (o & 255).astype(F32).astype(BF16)
+        hi = (o >> 8).astype(F32).astype(BF16)
+        ohl[:, at] = jnp.where(count == lo, one, nil)
+        v = loc_all[s]
+        for h in range(8):
+            lhs[pl.ds(16 * h, 16), at] = jnp.where(hi == h, v, nil[:16])
+    level2 = dot_nt(lhs[...], ohl[...])
+    for h in range(8):
+        lev_send[h // 2, :, pl.ds(256 * (h % 2), 256)] = level2[16 * h : 16 * h + 16, :].astype(BF16)
+
+    def send_lev(i, _):
+        ty = y_at(i)
+        rcopy(lev_send.at[ty], lev_recv.at[y], 4, g, ty * NZ + z).start()
+        return 0
+
+    lax.fori_loop(0, NY - 1, send_lev, 0)
+    lev_recv[y] = lev_send[y]
     wait_recv(bpk.at[pl.ds(0, NZ - 1)], 2)
-
-    def send_basis_y(i, _):
-        ts = ((y + far_first(i, NY)) % NY) * NZ + z
-        rcopy(bpk.at[rows], bpk.at[rows], 4, g, ts).start()
-        return 0
-
-    lax.fori_loop(0, NY - 1, send_basis_y, 0)
-
+    for k in range(NZ):
+        unpack(bpk, bfull, k)
+    wait_recv(lev_recv.at[pl.ds(0, NY - 1)], 4)
+    mine = lev_recv[0].astype(F32)
+    for k in range(1, NY):
+        mine = mine + lev_recv[k].astype(F32)
+    lev[y] = mine.astype(BF16)
+    p2[g * NY + y] = dot(lev[y], bfull[...]).astype(BF16)
+
+    def send_plane(o, _):
+        tg, ts = plane_peer(o)
+        rcopy(p2.at[g * NY + y], p2.at[g * NY + y], 5, tg, ts).start()
+        return 0
+
+    lax.fori_loop(0, plane - 1, send_plane, 0)
+
+    def send_level2(i, _):
+        rcopy(lev.at[y], lev.at[y], 3, g, y_at(i) * NZ + z).start()
+        return 0
+
+    lax.fori_loop(0, NY - 1, send_level2, 0)
+
+    def send_n(i, _):
+        tz = z_at(i)
+        rcopy(nsend.at[tz], npk.at[z], 11, g, y * NZ + tz).start()
+        return 0
+
+    lax.fori_loop(0, NZ - 1, send_n, 0)
     ld_coup.wait()
     ld_dir.wait()
     ld_inner.wait()
@@ -240,52 +280,14 @@
         sl = pl.ds(bi * k, bi)
         quick[k] = dot(coupling[k], dirichlet[k]).astype(BF16)
         inter[:, sl] = dot(inner[:, sl].astype(BF16), dirichlet[k])
-
-    wait_recv(own_all.at[pl.ds(0, nsub - NZ)], 3)
-
-    def masks(s, _):
-        o = own_all[s]
-        lo, hi = o & 255, o >> 8
-        ohl[:, pl.ds(pl.multiple_of(s * 128, 128), 128)] = (
-            (lax.broadcasted_iota(jnp.int32, (256, 128), 0) == lo).astype(F32).astype(BF16)
-        )
-        for h in range(8):
-            m = (hi == h).astype(F32)
-            hmask[s, pl.ds(16 * h, 16), :] = jnp.broadcast_to(m, (16, 128)).astype(BF16)
-        return 0
-
-    lax.fori_loop(0, nsub, masks, 0)
-
-    wait_recv(bpk.at[pl.ds(0, nsub - NZ)], 4)
-
-    def unpack_basis(q, _):
-        unpack(bpk, bfull, q)
-        return 0
-
-    lax.fori_loop(0, nsub, unpack_basis, 0)
-
-    wait_recv(loc_all.at[pl.ds(0, nsub - 1)], 0)
-    for s in range(nsub):
-        v = loc_all[s]
-        for h in range(8):
-            lhs[pl.ds(16 * h, 16), pl.ds(128 * s, 128)] = v * hmask[s, pl.ds(16 * h, 16), :]
-    level2 = dot_nt(lhs[...], ohl[...])
-    for h in range(8):
-        lev[:, pl.ds(256 * h, 256)] = level2[16 * h : 16 * h + 16, :].astype(BF16)
-    p2[g] = dot(lev[...], bfull[...]).astype(BF16)
-
-    def send_group(o, _):
-        rcopy(p2.at[g], p2.at[g], 5, (g + o) % ngroup, sub).start()
-        return 0
-
-    lax.fori_loop(1, ngroup, send_group, 0)
-    solved = dot_nt(lev[...], ginv_pad[...])
+    wait_recv(lev.at[pl.ds(0, NY - 1)], 3)
+    solved = dot_nt(jnp.concatenate([lev[k] for k in range(NY)], axis=1), ginv_pad[...])
     wait_recv(npk.at[pl.ds(0, NZ - 1)], 11)
     for k in range(NZ):
         unpack(npk, nz, k)
-    wait_recv(p2.at[pl.ds(0, ngroup - 1)], 5)
+    wait_recv(p2.at[pl.ds(0, plane - 1)], 5)
     level3 = p2[0].astype(F32)
-    for k in range(1, ngroup):
+    for k in range(1, plane):
         level3 = level3 + p2[k].astype(F32)
 
     part = dot_nt(level3.astype(BF16), nz[...])
@@ -294,7 +296,7 @@
         p3[z, pl.ds(16 * t, 16), :] = (part[:, 128 * t : 128 * t + 128] + own_part).astype(BF16)
 
     def send_part(i, _):
-        rcopy(p3.at[z], p3.at[z], 6, g, y * NZ + (z + far_first(i, NZ)) % NZ).start()
+        rcopy(p3.at[z], p3.at[z], 6, g, y * NZ + z_at(i)).start()
         return 0
 
     lax.fori_loop(0, NZ - 1, send_part, 0)
@@ -302,7 +304,7 @@
     def pick(t, _):
         at = pl.multiple_of(t * 256, 256)
         ohv[pl.ds(at, 256), :] = (
-            (lax.broadcasted_iota(jnp.int32, (256, 128), 0) + at == own_all[sub]).astype(F32).astype(BF16)
+            (lax.broadcasted_iota(jnp.int32, (256, 128), 0) + at == own_all[z]).astype(F32).astype(BF16)
         )
         return 0
 
@@ -319,7 +321,7 @@
     c2[y] = c2y.astype(BF16)
 
     def send_coarse(i, _):
-        rcopy(c2.at[y], c2.at[y], 7, g, ((y + far_first(i, NY)) % NY) * NZ + z).start()
+        rcopy(c2.at[y], c2.at[y], 7, g, y_at(i) * NZ + z).start()
         return 0
 
     lax.fori_loop(0, NY - 1, send_coarse, 0)
@@ -354,7 +356,7 @@
             dsend[first + i] = v.astype(BF16)
 
         def send_slot(o, _):
-            to = first + (z + far_first(o, NZ)) % NZ
+            to = first + z_at(o)
             rcopy(dsend.at[to], drecv.at[sub], 10, g, to).start()
             return 0
 
@@ -390,12 +392,12 @@
         sl = pl.ds(bi * k, bi)
         inter[:, sl] = inter[:, sl] - dot(block, quick[k])
 
-    wait_send(loc_all.at[pl.ds(0, nsub - 1)], 0)
+    wait_send(loc_all.at[pl.ds(0, NZ - 1)], 0)
     wait_send(own_all.at[pl.ds(0, NZ - 1)], 1)
+    wait_send(lev.at[pl.ds(0, NY - 1)], 3)
+    wait_send(lev_recv.at[pl.ds(0, NY - 1)], 4)
     wait_send(bpk.at[pl.ds(0, NZ - 1)], 2)
-    wait_send(own_all.at[pl.ds(0, nsub - NZ)], 3)
-    wait_send(bpk.at[pl.ds(0, nsub - NZ)], 4)
-    wait_send(p2.at[pl.ds(0, ngroup - 1)], 5)
+    wait_send(p2.at[pl.ds(0, plane - 1)], 5)
     wait_send(p3.at[pl.ds(0, NZ - 1)], 6)
     wait_send(c2.at[pl.ds(0, NY - 1)], 7)
     wait_send(npk.at[pl.ds(0, NZ - 1)], 11)
@@ -454,21 +456,22 @@
     work = [
         v((slots, 1, 128), F32),
         v((rows, width), BF16),
-        v((nsub, rows, 128), BF16),
-        v((nsub, 1, 128), jnp.int32),
+        v((NZ, rows, 128), BF16),
+        v((NZ, 1, 128), jnp.int32),
         v((NZ, 32, 128), BF16),
-        v((nsub, 32, 128), BF16),
-        v((group_width, 128), BF16),
-        v((256, 128 * nsub), BF16),
-        v((nsub, 128, 128), BF16),
-        v((128, 128 * nsub), BF16),
-        v((rows, group_width), BF16),
+        v((NZ, 32, 128), BF16),
+        v((64 * NZ, 128), BF16),
+        v((256, 128 * NZ), BF16),
+        v((128, 128 * NZ), BF16),
+        v((NY, rows, group_width // NY), BF16),
+        v((NY, rows, group_width // NY), BF16),
+        v((NY, rows, group_width // NY), BF16),
         v((group_width, 128), BF16),
         v((128, group_width), BF16),
         v((NZ, 32, 128), BF16),
         v((NZ, 32, 128), BF16),
         v((64 * NZ, 128), BF16),
-        v((ngroup, rows, 128), BF16),
+        v((ngroup * NY, rows, 128), BF16),
         v((NZ, rows * NZ // 2, 128), BF16),
         v((NY, rows * NZ // 2, 128), BF16),
         v((slots, rows, 128), F32),

time: 45.7 us -> 42.3 us (0.926)
  Pallas kernels: 43.5 us -> 40.1 us
    pallas_call x1, Pallas kernels: 43.5 us -> 40.1 us  [shards(): pl.pallas_call(functools.partial(kernel, ngroup, nsub), out_shape=(pltpu....]
where the time goes in v3:
time: 42.3 us; the launch traced here: 42.1 us
  Pallas kernels  40.1 us (95%)
  local copies, waits for them, and re-layouts  1.39 us (3%)
  between operations  0.64 us (2%)
    pallas_call x1, Pallas kernels, shards(): pl.pallas_call(functools.partial(kernel, ngroup, nsub), out_shape=(pltpu....  40.1 us
    unnamed x2, local copies, waits for them, and re-layouts  1.39 us

profile of v3, /device:TPU:32, one launch (start us, length us, event | category | flops | bytes accessed | tf_op | source)
XLA Modules:
  0.0 42.1 jit_solution(12340578485585158606)
XLA Ops:
  0.6 40.1 %bddc.1 = (f32[16,4352]{1,0:T(8,128)S(1)}, f32[16,3072]{1,0:T(8,128)S(1)}) custom-call(f32[16,4352]{1,0:T(8,128)} %bitcast.16, f32[16,3072]{1,0:T(8,128)} %bitcast.17, f32[1,4352]{1,0:T(1,128)} %weights_h.1, s32[1,32]{1,0:T(1,128)} %nbr_h.1, s32[1,128]{1,0:T(1,128)} %own_h.1, s32[1,8]{1,0:T(1,128)} %cidx_h.1, bf16[17,256,256]{2,1,0:T(8,128)(2,1)} %bitcast.12, ...), custom_call_target="tpu_custom_call" | custom-call | tf_op jit(solution)/shard_map/bddc/pallas_call | solution.py:491
  40.7 0.7 %copy.17 = f32[1,16,4352]{2,1,0:T(8,128)} copy(f32[1,16,4352]{2,1,0:T(8,128)S(1)} %bitcast.9) | data formatting | bytes 557056
  41.4 0.7 %copy.18 = f32[1,16,3072]{2,1,0:T(8,128)} copy(f32[1,16,3072]{2,1,0:T(8,128)S(1)} %bitcast.10) | data formatting | bytes 393216

commit v4 on v3

--- a/solution.py
+++ b/solution.py
@@ -110,8 +110,6 @@
     ]
     loads = [pltpu.make_async_copy(s, d, in_sem.at[i]) for i, (s, d) in enumerate(loads)]
     (ld_nbr, ld_w, ld_resid, ld_cb, ld_own, ld_basis, ld_neu, ld_top, ld_ginv, ld_cidx, ld_inner, ld_coup, ld_dir) = loads
-    for ld in (ld_cb, ld_resid, ld_nbr, ld_w, ld_basis, ld_own):
-        ld.start()
 
     def far_first(i, n):
         return n // 2 + jnp.where(i % 2 == 1, -((i + 1) // 2), i // 2)
@@ -138,6 +136,8 @@
         return 0
 
     lax.fori_loop(0, NZ - 1, greet_z, 0)
+    for ld in (ld_cb, ld_resid, ld_nbr, ld_w, ld_basis, ld_own):
+        ld.start()
     lax.fori_loop(0, plane - 1, greet_plane, 0)
 
     def rcopy(src, dst, phase, tg, ts):
@@ -214,6 +214,13 @@
     ld_top.wait()
     pack_z(dot(basis[...].astype(BF16), top[...].astype(BF16)), nsend)
     npk[z] = nsend[z]
+
+    def send_n(i, _):
+        tz = z_at(i)
+        rcopy(nsend.at[tz], npk.at[z], 11, g, y * NZ + tz).start()
+        return 0
+
+    lax.fori_loop(0, NZ - 1, send_n, 0)
     mine_rows = pl.ds(pl.multiple_of(par * 64, 64), 64)
     other_rows = pl.ds(pl.multiple_of((1 - par) * 64, 64), 64)
     ld_ginv.wait()
@@ -244,6 +251,7 @@
 
     lax.fori_loop(0, NY - 1, send_lev, 0)
     lev_recv[y] = lev_send[y]
+
     wait_recv(bpk.at[pl.ds(0, NZ - 1)], 2)
     for k in range(NZ):
         unpack(bpk, bfull, k)
@@ -267,19 +275,6 @@
 
     lax.fori_loop(0, NY - 1, send_level2, 0)
 
-    def send_n(i, _):
-        tz = z_at(i)
-        rcopy(nsend.at[tz], npk.at[z], 11, g, y * NZ + tz).start()
-        return 0
-
-    lax.fori_loop(0, NZ - 1, send_n, 0)
-    ld_coup.wait()
-    ld_dir.wait()
-    ld_inner.wait()
-    for k in range(ki):
-        sl = pl.ds(bi * k, bi)
-        quick[k] = dot(coupling[k], dirichlet[k]).astype(BF16)
-        inter[:, sl] = dot(inner[:, sl].astype(BF16), dirichlet[k])
     wait_recv(lev.at[pl.ds(0, NY - 1)], 3)
     solved = dot_nt(jnp.concatenate([lev[k] for k in range(NY)], axis=1), ginv_pad[...])
     wait_recv(npk.at[pl.ds(0, NZ - 1)], 11)
@@ -309,22 +304,22 @@
         return 0
 
     lax.fori_loop(0, 8, pick, 0)
+    wait_recv(p3.at[pl.ds(0, NZ - 1)], 6)
+    c2y = p3[0].astype(F32)
+    for k in range(1, NZ):
+        c2y = c2y + p3[k].astype(F32)
+    c2[y] = c2y.astype(BF16)
+
+    def send_coarse(i, _):
+        rcopy(c2.at[y], c2.at[y], 7, g, y_at(i) * NZ + z).start()
+        return 0
+
+    lax.fori_loop(0, NY - 1, send_coarse, 0)
     ld_neu.wait()
     for k in range(kn):
         v = dot(weighted[:, 256 * k : 256 * k + 256], neumann[k])
         nsc[2 * k] = v[:, :128] * scale[2 * k]
         nsc[2 * k + 1] = v[:, 128:] * scale[2 * k + 1]
-    wait_recv(p3.at[pl.ds(0, NZ - 1)], 6)
-    c2y = p3[0].astype(F32)
-    for k in range(1, NZ):
-        c2y = c2y + p3[k].astype(F32)
-    c2[y] = c2y.astype(BF16)
-
-    def send_coarse(i, _):
-        rcopy(c2.at[y], c2.at[y], 7, g, y_at(i) * NZ + z).start()
-        return 0
-
-    lax.fori_loop(0, NY - 1, send_coarse, 0)
     wait_recv(c2.at[pl.ds(0, NY - 1)], 7)
     coarse2 = jnp.concatenate(
         [c2[k, 16 * t : 16 * t + 16, :] for k in range(NY) for t in range(NZ // 2)], axis=1
@@ -362,6 +357,14 @@
 
         lax.fori_loop(0, NZ if c < NY - 1 else NZ - 1, send_slot, 0)
     drecv[sub] = dsend[sub]
+
+    ld_coup.wait()
+    ld_dir.wait()
+    ld_inner.wait()
+    for k in range(ki):
+        sl = pl.ds(bi * k, bi)
+        quick[k] = dot(coupling[k], dirichlet[k]).astype(BF16)
+        inter[:, sl] = dot(inner[:, sl].astype(BF16), dirichlet[k])
 
     @pl.when(g > 0)
     def _():
@@ -411,6 +414,17 @@
         to_lower.wait_send()
 
     wait_send(drecv.at[pl.ds(0, nsub - 1)], 10)
+
+
+def store(iface, inter, iface_h, inter_h, sem):
+    copies = [
+        pltpu.make_async_copy(iface, iface_h.at[0], sem.at[0]),
+        pltpu.make_async_copy(inter, inter_h.at[0], sem.at[1]),
+    ]
+    for c in copies:
+        c.start()
+    for c in copies:
+        c.wait()
 
 
 def shards(
@@ -502,7 +516,19 @@
         ),
         name="bddc",
     )(*ins)
-    return iface[None], inter[None]
+    iface, inter = pl.pallas_call(
+        store,
+        out_shape=(
+            jax.ShapeDtypeStruct((1, rows, width), F32),
+            jax.ShapeDtypeStruct((1, rows, inner_width), F32),
+        ),
+        in_specs=[anywhere] * 2,
+        out_specs=(anywhere, anywhere),
+        scratch_shapes=[pltpu.SemaphoreType.DMA((2,))],
+        compiler_params=pltpu.CompilerParams(vmem_limit_bytes=2**20),
+        name="store",
+    )(iface, inter)
+    return iface, inter
 
 
 def solution(mesh):

time: 42.3 us -> 41.7 us (0.986)
  local copies, waits for them, and re-layouts: 1.39 us -> 0 us
  Pallas kernels: 40.1 us -> 40.8 us
    unnamed x2 -> x0, local copies, waits for them, and re-layouts: 1.39 us -> none
    pallas_call x0 -> x1, Pallas kernels: none -> 0.79 us  [shards(): pl.pallas_call(store, out_shape=(jax.ShapeDtypeStruct((1, rows, width), F...]
where the time goes in v4:
time: 41.7 us; the launch traced here: 41.5 us
  Pallas kernels  40.8 us (98%)
  between operations  0.64 us (2%)
    pallas_call x1, Pallas kernels, shards(): pl.pallas_call(functools.partial(kernel, ngroup, nsub), out_shape=(pltpu....  40.1 us

profile of v4, /device:TPU:32, one launch (start us, length us, event | category | flops | bytes accessed | tf_op | source)
XLA Modules:
  0.0 41.5 jit_solution(10188302940123905956)
XLA Ops:
  0.6 40.1 %bddc.1 = (f32[16,4352]{1,0:T(8,128)S(1)}, f32[16,3072]{1,0:T(8,128)S(1)}) custom-call(f32[16,4352]{1,0:T(8,128)} %bitcast.12, f32[16,3072]{1,0:T(8,128)} %bitcast.13, f32[1,4352]{1,0:T(1,128)} %weights_h.1, s32[1,32]{1,0:T(1,128)} %nbr_h.1, s32[1,128]{1,0:T(1,128)} %own_h.1, s32[1,8]{1,0:T(1,128)} %cidx_h.1, bf16[17,256,256]{2,1,0:T(8,128)(2,1)} %bitcast.8, ...), custom_call_target="tpu_custom_call" | custom-call | tf_op jit(solution)/shard_map/bddc/pallas_call | solution.py:505
  40.7 0.8 %store.1 = (f32[1,16,4352]{2,1,0:T(8,128)}, f32[1,16,3072]{2,1,0:T(8,128)}) custom-call(f32[16,4352]{1,0:T(8,128)S(1)} %get-tuple-element.4.iface, f32[16,3072]{1,0:T(8,128)S(1)} %get-tuple-element.5.inter), custom_call_target="tpu_custom_call" | custom-call | tf_op jit(solution)/shard_map/store/pallas_call | solution.py:519

commit v5 on v4

--- a/solution.py
+++ b/solution.py
@@ -13,6 +13,7 @@
 NT = (((1,), (1,)), ((), ()))
 
 NY, NZ = 4, 8
+QZ = NZ // 2
 
 
 def dot(a, b):
@@ -58,7 +59,6 @@
     loc_all,
     own_all,
     bsend,
-    bpk,
     bfull,
     ohl,
     lhs,
@@ -68,7 +68,6 @@
     ohv,
     ginv_pad,
     nsend,
-    npk,
     nz,
     p2,
     p3,
@@ -156,23 +155,13 @@
     def wait_send(ref, phase):
         pltpu.make_async_copy(ref, ref, send_sem.at[phase]).wait()
 
-    lane = lax.broadcasted_iota(jnp.int32, (1, 128), 1)
-    low = lane < 64
-    def pack_z(src, dst):
-        for k in range(NZ):
-            t = slice(128 * (k // 2), 128 * (k // 2) + 128)
-            a, b = src[:32, t], src[32:, t]
-            if k % 2 == 0:
-                pk = jnp.where(low, a, pltpu.roll(b, 64, 1))
-            else:
-                pk = jnp.where(low, pltpu.roll(a, 64, 1), b)
-            dst[k] = pk.astype(BF16)
-
-    def unpack(src, dst, q):
-        p = src[q].astype(F32)
-        at = q * 64 if isinstance(q, int) else pl.multiple_of(q * 64, 64)
-        dst[pl.ds(at, 32), :] = jnp.where(low, p, 0.0).astype(BF16)
-        dst[pl.ds(at + 32, 32), :] = jnp.where(low, pltpu.roll(p, 64, 1), 0.0).astype(BF16)
+    k_mine, half = z % QZ, z // QZ
+    my_rows = pl.ds(pl.multiple_of(64 * z, 64), 64)
+    my_nz_rows = pl.ds(pl.multiple_of(64 * k_mine, 64), 64)
+
+    def tiles(src, dst):
+        for k in range(QZ):
+            dst[k] = src[:, 128 * k : 128 * k + 128].astype(BF16)
 
     ld_nbr.wait()
     ld_w.wait()
@@ -187,8 +176,8 @@
     ld_cb.wait()
     loc_all[z] = dot(weighted[...], cb[...]).astype(BF16)
     ld_basis.wait()
-    pack_z(basis[...], bsend)
-    bpk[z] = bsend[z]
+    tiles(basis[...], bsend)
+    bfull[my_rows, :] = bsend[k_mine]
     ld_own.wait()
 
     for ld in (ld_top, ld_ginv, ld_neu, ld_coup, ld_dir, ld_inner, ld_cidx):
@@ -206,21 +195,21 @@
 
     def send_z(i, _):
         tz = z_at(i)
-        rcopy(bsend.at[tz], bpk.at[z], 2, g, y * NZ + tz).start()
+        rcopy(bsend.at[tz % QZ], bfull.at[my_rows], 2, g, y * NZ + tz).start()
         return 0
 
     lax.fori_loop(0, NZ - 1, send_z, 0)
 
     ld_top.wait()
-    pack_z(dot(basis[...].astype(BF16), top[...].astype(BF16)), nsend)
-    npk[z] = nsend[z]
+    tiles(dot(basis[...].astype(BF16), top[...].astype(BF16)), nsend)
+    nz[my_nz_rows, :] = nsend[k_mine]
 
     def send_n(i, _):
-        tz = z_at(i)
-        rcopy(nsend.at[tz], npk.at[z], 11, g, y * NZ + tz).start()
-        return 0
-
-    lax.fori_loop(0, NZ - 1, send_n, 0)
+        k = (k_mine + i) % QZ
+        rcopy(nsend.at[k], nz.at[my_nz_rows], 11, g, y * NZ + half * QZ + k).start()
+        return 0
+
+    lax.fori_loop(1, QZ, send_n, 0)
     mine_rows = pl.ds(pl.multiple_of(par * 64, 64), 64)
     other_rows = pl.ds(pl.multiple_of((1 - par) * 64, 64), 64)
     ld_ginv.wait()
@@ -252,9 +241,7 @@
     lax.fori_loop(0, NY - 1, send_lev, 0)
     lev_recv[y] = lev_send[y]
 
-    wait_recv(bpk.at[pl.ds(0, NZ - 1)], 2)
-    for k in range(NZ):
-        unpack(bpk, bfull, k)
+    wait_recv(bfull.at[pl.ds(0, 64 * (NZ - 1))], 2)
     wait_recv(lev_recv.at[pl.ds(0, NY - 1)], 4)
     mine = lev_recv[0].astype(F32)
     for k in range(1, NY):
@@ -275,19 +262,25 @@
 
     lax.fori_loop(0, NY - 1, send_level2, 0)
 
+    ld_coup.wait()
+    ld_dir.wait()
+    ld_inner.wait()
+    for k in range(ki):
+        sl = pl.ds(bi * k, bi)
+        quick[k] = dot(coupling[k], dirichlet[k]).astype(BF16)
+        inter[:, sl] = dot(inner[:, sl].astype(BF16), dirichlet[k])
+
     wait_recv(lev.at[pl.ds(0, NY - 1)], 3)
     solved = dot_nt(jnp.concatenate([lev[k] for k in range(NY)], axis=1), ginv_pad[...])
-    wait_recv(npk.at[pl.ds(0, NZ - 1)], 11)
-    for k in range(NZ):
-        unpack(npk, nz, k)
+    wait_recv(nz.at[pl.ds(0, 64 * (QZ - 1))], 11)
     wait_recv(p2.at[pl.ds(0, plane - 1)], 5)
     level3 = p2[0].astype(F32)
     for k in range(1, plane):
         level3 = level3 + p2[k].astype(F32)
 
     part = dot_nt(level3.astype(BF16), nz[...])
-    for t in range(NZ // 2):
-        own_part = jnp.where(z // 2 == t, solved, 0.0)
+    for t in range(QZ // 2):
+        own_part = jnp.where(z // 2 % 2 == t, solved, 0.0)
         p3[z, pl.ds(16 * t, 16), :] = (part[:, 128 * t : 128 * t + 128] + own_part).astype(BF16)
 
     def send_part(i, _):
@@ -305,10 +298,11 @@
 
     lax.fori_loop(0, 8, pick, 0)
     wait_recv(p3.at[pl.ds(0, NZ - 1)], 6)
-    c2y = p3[0].astype(F32)
-    for k in range(1, NZ):
-        c2y = c2y + p3[k].astype(F32)
-    c2[y] = c2y.astype(BF16)
+    for h in range(2):
+        c2y = p3[QZ * h].astype(F32)
+        for k in range(1, QZ):
+            c2y = c2y + p3[QZ * h + k].astype(F32)
+        c2[y, pl.ds(32 * h, 32), :] = c2y.astype(BF16)
 
     def send_coarse(i, _):
         rcopy(c2.at[y], c2.at[y], 7, g, y_at(i) * NZ + z).start()
@@ -358,13 +352,6 @@
         lax.fori_loop(0, NZ if c < NY - 1 else NZ - 1, send_slot, 0)
     drecv[sub] = dsend[sub]
 
-    ld_coup.wait()
-    ld_dir.wait()
-    ld_inner.wait()
-    for k in range(ki):
-        sl = pl.ds(bi * k, bi)
-        quick[k] = dot(coupling[k], dirichlet[k]).astype(BF16)
-        inter[:, sl] = dot(inner[:, sl].astype(BF16), dirichlet[k])
 
     @pl.when(g > 0)
     def _():
@@ -399,11 +386,11 @@
     wait_send(own_all.at[pl.ds(0, NZ - 1)], 1)
     wait_send(lev.at[pl.ds(0, NY - 1)], 3)
     wait_send(lev_recv.at[pl.ds(0, NY - 1)], 4)
-    wait_send(bpk.at[pl.ds(0, NZ - 1)], 2)
+    wait_send(bfull.at[pl.ds(0, 64 * (NZ - 1))], 2)
     wait_send(p2.at[pl.ds(0, plane - 1)], 5)
     wait_send(p3.at[pl.ds(0, NZ - 1)], 6)
     wait_send(c2.at[pl.ds(0, NY - 1)], 7)
-    wait_send(npk.at[pl.ds(0, NZ - 1)], 11)
+    wait_send(nz.at[pl.ds(0, 64 * (QZ - 1))], 11)
 
     @pl.when(g < ngroup - 1)
     def _():
@@ -472,8 +459,7 @@
         v((rows, width), BF16),
         v((NZ, rows, 128), BF16),
         v((NZ, 1, 128), jnp.int32),
-        v((NZ, 32, 128), BF16),
-        v((NZ, 32, 128), BF16),
+        v((QZ, 64, 128), BF16),
         v((64 * NZ, 128), BF16),
         v((256, 128 * NZ), BF16),
         v((128, 128 * NZ), BF16),
@@ -482,11 +468,10 @@
         v((NY, rows, group_width // NY), BF16),
         v((group_width, 128), BF16),
         v((128, group_width), BF16),
-        v((NZ, 32, 128), BF16),
-        v((NZ, 32, 128), BF16),
-        v((64 * NZ, 128), BF16),
+        v((QZ, 64, 128), BF16),
+        v((64 * QZ, 128), BF16),
         v((ngroup * NY, rows, 128), BF16),
-        v((NZ, rows * NZ // 2, 128), BF16),
+        v((NZ, rows * QZ // 2, 128), BF16),
         v((NY, rows * NZ // 2, 128), BF16),
         v((slots, rows, 128), F32),
         v((slots, rows, 128), F32),

time: 41.7 us -> 41.6 us (level)
  no operation moved by 1% of the time
where the time goes in v5:
time: 41.6 us
  Pallas kernels  40.9 us (98%)
  between operations  0.64 us (2%)
    pallas_call x1, Pallas kernels, shards(): pl.pallas_call(functools.partial(kernel, ngroup, nsub), out_shape=(pltpu....  40.1 us

profile of v5, /device:TPU:32, one launch (start us, length us, event | category | flops | bytes accessed | tf_op | source)
XLA Modules:
  0.0 41.6 jit_solution(7488873649032287655)
XLA Ops:
  0.6 40.1 %bddc.1 = (f32[16,4352]{1,0:T(8,128)S(1)}, f32[16,3072]{1,0:T(8,128)S(1)}) custom-call(f32[16,4352]{1,0:T(8,128)} %bitcast.12, f32[16,3072]{1,0:T(8,128)} %bitcast.13, f32[1,4352]{1,0:T(1,128)} %weights_h.1, s32[1,32]{1,0:T(1,128)} %nbr_h.1, s32[1,128]{1,0:T(1,128)} %own_h.1, s32[1,8]{1,0:T(1,128)} %cidx_h.1, bf16[17,256,256]{2,1,0:T(8,128)(2,1)} %bitcast.8, ...), custom_call_target="tpu_custom_call" | custom-call | tf_op jit(solution)/shard_map/bddc/pallas_call | solution.py:490
  40.8 0.8 %store.1 = (f32[1,16,4352]{2,1,0:T(8,128)}, f32[1,16,3072]{2,1,0:T(8,128)}) custom-call(f32[16,4352]{1,0:T(8,128)S(1)} %get-tuple-element.4.iface, f32[16,3072]{1,0:T(8,128)S(1)} %get-tuple-element.5.inter), custom_call_target="tpu_custom_call" | custom-call | tf_op jit(solution)/shard_map/store/pallas_call | solution.py:504

commit v6 on v5

--- a/solution.py
+++ b/solution.py
@@ -262,13 +262,16 @@
 
     lax.fori_loop(0, NY - 1, send_level2, 0)
 
+    def prepare(first, last):
+        for k in range(first, last):
+            sl = pl.ds(bi * k, bi)
+            quick[k] = dot(coupling[k], dirichlet[k]).astype(BF16)
+            inter[:, sl] = dot(inner[:, sl].astype(BF16), dirichlet[k])
+
     ld_coup.wait()
     ld_dir.wait()
     ld_inner.wait()
-    for k in range(ki):
-        sl = pl.ds(bi * k, bi)
-        quick[k] = dot(coupling[k], dirichlet[k]).astype(BF16)
-        inter[:, sl] = dot(inner[:, sl].astype(BF16), dirichlet[k])
+    prepare(0, ki // 4)
 
     wait_recv(lev.at[pl.ds(0, NY - 1)], 3)
     solved = dot_nt(jnp.concatenate([lev[k] for k in range(NY)], axis=1), ginv_pad[...])
@@ -297,6 +300,7 @@
         return 0
 
     lax.fori_loop(0, 8, pick, 0)
+    prepare(ki // 4, 3 * ki // 4)
     wait_recv(p3.at[pl.ds(0, NZ - 1)], 6)
     for h in range(2):
         c2y = p3[QZ * h].astype(F32)
@@ -314,26 +318,12 @@
         v = dot(weighted[:, 256 * k : 256 * k + 256], neumann[k])
         nsc[2 * k] = v[:, :128] * scale[2 * k]
         nsc[2 * k + 1] = v[:, 128:] * scale[2 * k + 1]
+    prepare(3 * ki // 4, ki)
     wait_recv(c2.at[pl.ds(0, NY - 1)], 7)
     coarse2 = jnp.concatenate(
         [c2[k, 16 * t : 16 * t + 16, :] for k in range(NY) for t in range(NZ // 2)], axis=1
     )
     values = dot(coarse2, ohv[...]).astype(BF16)
-
-    spread = dot_nt(values, cb[pl.ds(128 * nsub, 256), :])
-    for i in range(2):
-        scaled[nsub + i] = nsc[nsub + i] + scale[nsub + i] * spread[:, 128 * i : 128 * i + 128]
-
-    to_upper = rcopy(scaled.at[nsub + 1], face.at[0], 8, jnp.minimum(g + 1, ngroup - 1), sub)
-    to_lower = rcopy(scaled.at[nsub], face.at[1], 9, jnp.maximum(g - 1, 0), sub)
-
-    @pl.when(g < ngroup - 1)
-    def _():
-        to_upper.start()
-
-    @pl.when(g > 0)
-    def _():
-        to_lower.start()
 
     for c in range(NY):
         ty = (y + (2, 1, 3, 0)[c]) % NY
@@ -350,6 +340,22 @@
             return 0
 
         lax.fori_loop(0, NZ if c < NY - 1 else NZ - 1, send_slot, 0)
+
+    spread = dot_nt(values, cb[pl.ds(128 * nsub, 256), :])
+    for i in range(2):
+        scaled[nsub + i] = nsc[nsub + i] + scale[nsub + i] * spread[:, 128 * i : 128 * i + 128]
+
+    to_upper = rcopy(scaled.at[nsub + 1], face.at[0], 8, jnp.minimum(g + 1, ngroup - 1), sub)
+    to_lower = rcopy(scaled.at[nsub], face.at[1], 9, jnp.maximum(g - 1, 0), sub)
+
+    @pl.when(g < ngroup - 1)
+    def _():
+        to_upper.start()
+
+    @pl.when(g > 0)
+    def _():
+        to_lower.start()
+
     drecv[sub] = dsend[sub]
 
 

time: 41.6 us -> 41.5 us (level)
  no operation moved by 1% of the time
where the time goes in v6:
time: 41.5 us; the launch traced here: 41.4 us
  Pallas kernels  40.8 us (98%)
  between operations  0.64 us (2%)
    pallas_call x1, Pallas kernels, shards(): pl.pallas_call(functools.partial(kernel, ngroup, nsub), out_shape=(pltpu....  40 us

profile of v6, /device:TPU:32, one launch (start us, length us, event | category | flops | bytes accessed | tf_op | source)
XLA Modules:
  0.0 41.4 jit_solution(8838108187148642392)
XLA Ops:
  0.6 40.0 %bddc.1 = (f32[16,4352]{1,0:T(8,128)S(1)}, f32[16,3072]{1,0:T(8,128)S(1)}) custom-call(f32[16,4352]{1,0:T(8,128)} %bitcast.12, f32[16,3072]{1,0:T(8,128)} %bitcast.13, f32[1,4352]{1,0:T(1,128)} %weights_h.1, s32[1,32]{1,0:T(1,128)} %nbr_h.1, s32[1,128]{1,0:T(1,128)} %own_h.1, s32[1,8]{1,0:T(1,128)} %cidx_h.1, bf16[17,256,256]{2,1,0:T(8,128)(2,1)} %bitcast.8, ...), custom_call_target="tpu_custom_call" | custom-call | tf_op jit(solution)/shard_map/bddc/pallas_call | solution.py:496
  40.6 0.8 %store.1 = (f32[1,16,4352]{2,1,0:T(8,128)}, f32[1,16,3072]{2,1,0:T(8,128)}) custom-call(f32[16,4352]{1,0:T(8,128)S(1)} %get-tuple-element.4.iface, f32[16,3072]{1,0:T(8,128)S(1)} %get-tuple-element.5.inter), custom_call_target="tpu_custom_call" | custom-call | tf_op jit(solution)/shard_map/store/pallas_call | solution.py:510
